TPU v7x, 256 devices: a whole 4x4x8 slice. The times are simulated.
256 devices in a mesh: context: 32 (over z, y), tensor: 8 (over x, core).
Axes of the slice: x: 4, y: 4, z: 8, core: 2. Of those that a mesh axis runs over, the one named last changes fastest.
Arguments:
- tokens: bfloat16 [24576, 4096], P('context', 'tensor'), may hold values from -6 to 6
- w_gate: bfloat16 [4096, 4096], P('context', 'tensor'), may hold values from -0.09375 to 0.09375
- w_value: bfloat16 [4096, 4096], P('context', 'tensor'), may hold values from -0.09375 to 0.09375
- w_keys: bfloat16 [4096, 2048], P('context', 'tensor'), may hold values from -0.09375 to 0.09375
- conv_value: float32 [4, 4096], P(None, 'tensor'), may hold values from -3 to 3
- key_filter_taps: float32 [4, 2048], P(None, 'tensor'), may hold values from -3 to 3
- step: float32 [24576, 64], P('context', 'tensor'), may hold values from 0 to 0.3
- decay_rate: float32 [64], P('tensor'), may hold values from 0.5 to 1.5
- skip: float32 [64], P('tensor'), may hold values from 0.1 to 0.5
- norm_gain: float32 [4096], P('tensor'), may hold values from 0.1 to 1.9
- w_out: bfloat16 [4096, 4096], P('tensor', 'context'), may hold values from -0.09375 to 0.09375
Outputs:
- mixed: bfloat16 [24576, 4096], P('context', 'tensor')
All inputs are finite; a program needn't handle non-finite values.
Results may differ from a plain program's by a relative error of at most 0.023.
Values may be sent and summed in bfloat16 or wider, within the bound.
No kernel may reach another device: no remote copies, remote signals or barrier semaphores. Data moves between devices by JAX's collectives and lax.ppermute only.
A program may use at most 128 MiB of HBM per device.

v0:
```python
import jax
import jax.numpy as jnp
from jax import lax
from jax.sharding import PartitionSpec as P

P_SIZE = 64
N = 128
BLOCK = 256


def passed_along(block, axis, distance):
    devices = range(lax.axis_size(axis))
    route = [(i - distance, i) for i in devices if i - distance in devices]
    return lax.ppermute(block, axis, route)


def prefix(array, axis, join, neutral):
    place = lax.axis_index(axis)
    gathered = jax.tree.map(
        lambda a, kind: lax.all_gather(a.astype(kind), axis), array, (jnp.bfloat16, jnp.bfloat16)
    )
    state = jax.tree.map(lambda a, e: jnp.zeros_like(a) + jnp.asarray(e, a.dtype), array, neutral)

    def one(turn, state):
        return join(
            state,
            jax.tree.map(
                lambda a, own: lax.dynamic_index_in_dim(a, turn, 0, False).astype(own.dtype),
                gathered,
                array,
            ),
        )

    return lax.fori_loop(0, place, one, state)


def ssd_blocks(signal, write_key, read_key, steps, forgetting_exponent, state, per_group):
    count = signal.shape[0] // BLOCK
    highest = lax.Precision.HIGHEST

    def fold(carry, block):
        block_signature, block_write, block_read, block_step, block_decay = block
        running = jnp.cumsum(block_decay, axis=0)
        spread_log = running[:, None, :] - running[None, :, :]
        lower = (jnp.arange(BLOCK)[:, None] >= jnp.arange(BLOCK)[None, :])[:, :, None]
        weights = (
            jnp.where(lower, jnp.exp(jnp.where(lower, spread_log, 0.0)), 0.0)
            * block_step[None, :, :]
        )
        scores = jnp.einsum(
            "sgn,rgn->gsr",
            block_read.astype(jnp.bfloat16),
            block_write.astype(jnp.bfloat16),
            preferred_element_type=jnp.float32,
        )
        scores = jnp.repeat(scores, per_group, axis=0) * jnp.transpose(weights, (2, 0, 1))
        result = jnp.einsum("hsr,rhp->shp", scores, block_signature, precision=highest)
        read_head = jnp.repeat(block_read, per_group, axis=1)
        emitting_channel = jnp.repeat(block_write, per_group, axis=1)
        result = result + jnp.exp(running)[:, :, None] * jnp.einsum(
            "shn,hpn->shp", read_head, carry, precision=highest
        )
        tail_weight = jnp.exp(running[-1][None, :] - running) * block_step
        fresh = jnp.exp(running[-1])[:, None, None] * carry + jnp.einsum(
            "rh,rhp,rhn->hpn", tail_weight, block_signature, emitting_channel, precision=highest
        )
        return (fresh, result)

    def split_blocks(array):
        return array.reshape((count, BLOCK) + array.shape[1:])

    blocks = (
        split_blocks(signal),
        split_blocks(write_key),
        split_blocks(read_key),
        split_blocks(steps),
        split_blocks(forgetting_exponent),
    )
    final, outputs = lax.scan(fold, state, blocks)
    return (outputs.reshape(signal.shape), final)


def local(
    tokens,
    w_gate,
    w_value,
    w_keys,
    conv_value,
    key_filter_taps,
    step,
    decay_rate,
    skip,
    norm_gain,
    w_out,
):
    whole = lax.all_gather(tokens, "tensor", axis=1, tiled=True)
    rows = whole.shape[0]
    first = jnp.dot(
        whole,
        lax.all_gather(w_gate, "context", axis=0, tiled=True),
        preferred_element_type=jnp.float32,
    )
    second_piece = jnp.dot(
        whole,
        lax.all_gather(w_value, "context", axis=0, tiled=True),
        preferred_element_type=jnp.float32,
    )
    third = jnp.dot(
        whole,
        lax.all_gather(w_keys, "context", axis=0, tiled=True),
        preferred_element_type=jnp.float32,
    )
    gate = first.astype(jnp.bfloat16)
    raw = jnp.concatenate([second_piece, third], axis=1).astype(jnp.bfloat16)
    taps = jnp.concatenate([conv_value, key_filter_taps], axis=1)
    reach = taps.shape[0] - 1
    before = passed_along(raw[rows - reach :], "context", 1)
    padded = jnp.concatenate([before, raw], axis=0).astype(jnp.float32)
    summed = jnp.zeros((rows, raw.shape[1]), jnp.float32)
    for tap in range(taps.shape[0]):
        summed = summed + taps[tap][None, :] * padded[tap : tap + rows]
    convolved = jax.nn.silu(summed).astype(jnp.bfloat16)
    local_heads = step.shape[1]
    width = local_heads * P_SIZE
    local_groups = w_keys.shape[1] // (2 * N)
    per_group = local_heads // local_groups
    signal = convolved[:, :width].astype(jnp.float32).reshape(rows, local_heads, P_SIZE)
    both_keys = convolved[:, width:].astype(jnp.float32).reshape(rows, local_groups, 2, N)
    read_key = both_keys[:, :, 1]
    forgetting_exponent = -step * decay_rate[None, :]
    start_state = jnp.zeros((local_heads, P_SIZE, N), jnp.float32)
    output, own_state = ssd_blocks(
        signal, both_keys[:, :, 0], read_key, step, forgetting_exponent, start_state, per_group
    )
    running = jnp.cumsum(forgetting_exponent, axis=0)
    piece_total = running[-1]

    def combine(earlier, later):
        return (earlier[0] + later[0], jnp.exp(later[0])[:, None, None] * earlier[1] + later[1])

    identity = (jnp.zeros_like(piece_total), jnp.zeros_like(own_state))
    incoming = prefix((piece_total, own_state), "context", combine, identity)[1]
    read_head = jnp.repeat(read_key, per_group, axis=1)
    state_correction = jnp.einsum(
        "shn,hpn->shp", read_head, incoming, precision=lax.Precision.HIGHEST
    )
    output = output + jnp.exp(running)[:, :, None] * state_correction + skip[None, :, None] * signal
    gated = output.reshape(rows, width) * jax.nn.silu(gate.astype(jnp.float32))
    grouped = gated.reshape(rows, local_groups, width // local_groups)
    reciprocal = lax.rsqrt(jnp.mean(grouped * grouped, axis=-1, keepdims=True) + 1e-05)
    normed = ((grouped * reciprocal).reshape(rows, width) * norm_gain[None, :]).astype(jnp.bfloat16)
    terms = jnp.dot(
        normed,
        lax.all_gather(w_out, "context", axis=1, tiled=True),
        preferred_element_type=jnp.float32,
    )
    return lax.psum_scatter(terms.astype(jnp.bfloat16), "tensor", scatter_dimension=1, tiled=True)


def solution(mesh):
    return jax.shard_map(
        local,
        mesh=mesh,
        in_specs=(
            P("context", "tensor"),
            P("context", "tensor"),
            P("context", "tensor"),
            P("context", "tensor"),
            P(None, "tensor"),
            P(None, "tensor"),
            P("context", "tensor"),
            P("tensor"),
            P("tensor"),
            P("tensor"),
            P("tensor", "context"),
        ),
        out_specs=P("context", "tensor"),
        check_vma=False,
    )
```

profile of v0, /device:TPU:1, one launch (start us, length us, event | category | flops | bytes accessed | tf_op | source)
XLA Modules:
  0.0 619.7 jit_solution(672814757393832227)
XLA Ops:
  10.2 1.4 negate_multiply_fusion
  11.6 81.4 %all-gather.11.cloned.1.call-done = bf16[4096,512]{1,0:T(8,128)(2,1)} async-done(((bf16[128,512]{1,0:T(8,128)(2,1)}), bf16[4096,512]{1,0:T(8,128)(2,1)}) %all-gather.11.cloned.1.call-update) | async-done | bytes 4194320 | tf_op jit(solution)/shard_map/all_gather | solution.py:105
  93.0 45.6 %all-gather.9.cloned.1.call-done = bf16[768,4096]{1,0:T(8,128)(2,1)} async-done(((bf16[768,512]{1,0:T(8,128)(2,1)}), bf16[768,4096]{1,0:T(8,128)(2,1)}) %all-gather.9.cloned.1.call-update) | async-done | bytes 6291472 | tf_op jit(solution)/shard_map/all_gather | solution.py:96
  138.6 7.5 %convolution_convert_fusion.2 = bf16[768,512]{0,1:T(8,128)(2,1)S(1)} fusion(bf16[768,4096]{1,0:T(8,128)(2,1)} %all-gather.9.cloned.1.call-done, bf16[4096,512]{1,0:T(8,128)(2,1)} %all-gather.11.cloned.1.call-done), kind=kOutput, calls=%fused_computation.71 | convolution fusion | flops 3221618688 | bytes 11272192 | tf_op jit(solution)/shard_map/dot_general | solution.py:103
  146.1 68.9 %all-gather.13.cloned.1.call-done = bf16[4096,256]{1,0:T(8,128)(2,1)} async-done(((bf16[128,256]{1,0:T(8,128)(2,1)}), bf16[4096,256]{1,0:T(8,128)(2,1)}) %all-gather.13.cloned.1.call-update) | async-done | bytes 2097168 | tf_op jit(solution)/shard_map/all_gather | solution.py:110
  215.0 5.2 convolution_convert_fusion.3
  220.3 2.3 collective-permute-start
  222.7 2.3 collective-permute-done
  225.7 2.6 multiply_convert_fusion
  230.4 1.8 reshape_reshape.3
  232.2 74.9 %while.26 = (s32[]{:T(128)}, f32[8,64,128]{2,1,0:T(8,128)S(1)}, f32[3,256,8,64]{1,0,3,2:T(4,128)}, f32[3,256,8]{1,2,0:T(8,128)}, f32[3,256,8]{1,2,0:T(8,128)}, /...) while((s32[]{:T(128)}, f32[8,64,128]{2,1,0:T(8,128)S(1)}, ...), condition=%wide.region_3.4_spmd.clone, body=%wide.region_0.3_spmd.clone.sunk | while | flops 825694208 | bytes 8275832 | solution.py:79
  234.9 2.1 constant_dynamic-slice_fusion.2
  237.7 2.6 fusion.81
  243.1 12.3 %dynamic_update_slice.6 = f32[3,256,8,64]{1,0,3,2:T(4,128)} dynamic-update-slice(f32[3,256,8,64]{1,0,3,2:T(4,128)} %get-tuple-element.311, f32[1,256,8,64]{1,0,3,2:T(1,128)S(1)} %copy.71, s32[]{:T(128)} %get-tuple-element.309, s32[]{:T(128)} %constant.54.clone.1..sunk.1, s32[]{:T(128)} %constant.54.clone.1..sunk.1, s32[]{:T(128)} %constant.54.clone.1..sunk.1) | dynamic-update-slice | bytes 1048580 | tf_op jit(solution)/shard_map/while/body/jit(dynamic_update_index_in_dim)/dynamic_update_slice | solution.py:79
  259.9 2.1 constant_dynamic-slice_fusion.2
  262.7 2.6 fusion.81
  266.4 1.2 fusion.82
  268.1 12.3 %dynamic_update_slice.6 = f32[3,256,8,64]{1,0,3,2:T(4,128)} dynamic-update-slice(f32[3,256,8,64]{1,0,3,2:T(4,128)} %get-tuple-element.311, f32[1,256,8,64]{1,0,3,2:T(1,128)S(1)} %copy.71, s32[]{:T(128)} %get-tuple-element.309, s32[]{:T(128)} %constant.54.clone.1..sunk.1, s32[]{:T(128)} %constant.54.clone.1..sunk.1, s32[]{:T(128)} %constant.54.clone.1..sunk.1) | dynamic-update-slice | bytes 1048580 | tf_op jit(solution)/shard_map/while/body/jit(dynamic_update_index_in_dim)/dynamic_update_slice | solution.py:79
  284.8 2.1 constant_dynamic-slice_fusion.2
  287.7 2.6 fusion.81
  291.4 1.2 fusion.82
  293.1 12.3 %dynamic_update_slice.6 = f32[3,256,8,64]{1,0,3,2:T(4,128)} dynamic-update-slice(f32[3,256,8,64]{1,0,3,2:T(4,128)} %get-tuple-element.311, f32[1,256,8,64]{1,0,3,2:T(1,128)S(1)} %copy.71, s32[]{:T(128)} %get-tuple-element.309, s32[]{:T(128)} %constant.54.clone.1..sunk.1, s32[]{:T(128)} %constant.54.clone.1..sunk.1, s32[]{:T(128)} %constant.54.clone.1..sunk.1) | dynamic-update-slice | bytes 1048580 | tf_op jit(solution)/shard_map/while/body/jit(dynamic_update_index_in_dim)/dynamic_update_slice | solution.py:79
  309.9 1.7 reduce-window.16
  312.9 33.7 %all-gather.1 = bf16[32,1,8]{2,1,0:T(2,128)(2,1)S(1)} all-gather(bf16[1,1,8]{2,1,0:T(2,128)(2,1)S(1)} %bitcast.134), channel_id=1, replica_groups=mesh['context'=32,'tensor'=8] {'context'}, dimensions={0}, use_global_device_ids=true | all-gather | bytes 528 | tf_op jit(solution)/shard_map/all_gather | solution.py:20
  347.5 2.9 reshape.128
  352.4 40.9 %all-gather.19.cloned.1.call-done = bf16[256,64,128]{2,1,0:T(8,128)(2,1)} async-done(((bf16[8,64,128]{2,1,0:T(8,128)(2,1)}), bf16[256,64,128]{2,1,0:T(8,128)(2,1)}) %all-gather.19.cloned.1.call-update) | async-done | bytes 4194320 | tf_op jit(solution)/shard_map/all_gather | solution.py:20
  393.6 5.5 fusion.42
  399.2 75.7 %all-gather.15.cloned.1.call-done = bf16[4096,512]{1,0:T(8,128)(2,1)} async-done(((bf16[128,512]{1,0:T(8,128)(2,1)}), bf16[4096,512]{1,0:T(8,128)(2,1)}) %all-gather.15.cloned.1.call-update) | async-done | bytes 4194320 | tf_op jit(solution)/shard_map/all_gather | solution.py:100
  474.9 8.2 %multiply_reduce_fusion = (f32[768]{0:T(1024)S(1)}, f32[768,512]{0,1:T(8,128)S(1)}) fusion(bf16[768,4096]{1,0:T(8,128)(2,1)} %all-gather.9.cloned.1.call-done, bf16[4096,512]{1,0:T(8,128)(2,1)} %all-gather.15.cloned.1.call-done, f32[768,8,64]{0,2,1:T(8,128)} %fusion.42), kind=kOutput, calls=%fused_computation.67 | convolution fusion | flops 3224763648 | bytes 13634560 | tf_op jit(solution)/shard_map/dot_general | solution.py:98
  483.1 74.0 %all-gather.17.cloned.1.call-done = bf16[512,4096]{1,0:T(8,128)(2,1)} async-done(((bf16[512,128]{1,0:T(8,128)(2,1)}), bf16[512,4096]{1,0:T(8,128)(2,1)}) %all-gather.17.cloned.1.call-update) | async-done | bytes 4194320 | tf_op jit(solution)/shard_map/all_gather | solution.py:154
  557.1 7.7 %convolution_convert_fusion = bf16[768,4096]{1,0:T(8,128)(2,1)} fusion(bf16[512,4096]{1,0:T(8,128)(2,1)} %all-gather.17.cloned.1.call-done, f32[768,512]{0,1:T(8,128)S(1)} %get-tuple-element.208, f32[512]{0:T(512)S(1)} %copy-done.2, f32[768]{0:T(1024)S(1)} %add_rsqrt_fusion), kind=kOutput, calls=%fused_computation.48 | convolution fusion | flops 3225550848 | bytes 12063744 | tf_op jit(solution)/shard_map/dot_general | solution.py:152
  564.9 48.0 %reduce-scatter.2.cloned.1.call-done = bf16[768,512]{1,0:T(8,128)(2,1)} async-done(((bf16[768,4096]{1,0:T(8,128)(2,1)}), bf16[768,512]{1,0:T(8,128)(2,1)}) %reduce-scatter.2.cloned.1.call-update) | async-done | bytes 786448 | tf_op jit(solution)/shard_map/reduce_scatter | solution.py:157
  (96 shorter events, 34.9 us)
Async XLA Ops:
  6.5 86.4 %all-gather.11.cloned.1.call-start = ((), (), s32[]{:S(2)}) async-start(), calls=%async_computation.2 | async-start | bytes 4325376 | tf_op jit(solution)/shard_map/all_gather | solution.py:105
  7.3 131.3 %all-gather.9.cloned.1.call-start = ((), (), s32[]{:S(2)}) async-start(), calls=%async_computation.1 | async-start | bytes 7077888 | tf_op jit(solution)/shard_map/all_gather | solution.py:96
  8.0 206.9 %all-gather.13.cloned.1.call-start = ((), (), s32[]{:S(2)}) async-start(), calls=%async_computation.3 | async-start | bytes 2162688 | tf_op jit(solution)/shard_map/all_gather | solution.py:110
  8.7 384.6 %all-gather.19.cloned.1.call-start = ((), (), s32[]{:S(2)}) async-start(), calls=%async_computation.7 | async-start | bytes 4325376 | tf_op jit(solution)/shard_map/all_gather | solution.py:20
  220.3 4.7 collective-permute-start
  307.8 167.1 %all-gather.15.cloned.1.call-start = ((), (), s32[]{:S(2)}) async-start(), calls=%async_computation.4 | async-start | bytes 4325376 | tf_op jit(solution)/shard_map/all_gather | solution.py:100
  308.4 248.7 %all-gather.17.cloned.1.call-start = ((), (), s32[]{:S(2)}) async-start(), calls=%async_computation.5 | async-start | bytes 4325376 | tf_op jit(solution)/shard_map/all_gather | solution.py:154
  309.0 303.9 %reduce-scatter.2.cloned.1.call-start = ((), (), s32[]{:S(2)}) async-start(), calls=%async_computation.6 | async-start | bytes 7077888 | tf_op jit(solution)/shard_map/reduce_scatter | solution.py:157
  351.5 42.1 %copy-start.1 = (f32[8]{0:T(128)S(1)}, f32[8]{0:T(128)}, u32[]{:S(2)}) copy-start(f32[8]{0:T(128)} %param.23) | copy-start | bytes 100
  352.4 41.2 %copy-start = (f32[768,8]{0,1:T(8,128)S(1)}, f32[768,8]{0,1:T(8,128)}, u32[]{:S(2)}) copy-start(f32[768,8]{0,1:T(8,128)} %get-tuple-element.205) | copy-start | bytes 73732
  399.2 158.0 %copy-start.2 = (f32[512]{0:T(512)S(1)}, f32[512]{0:T(512)}, u32[]{:S(2)}) copy-start(f32[512]{0:T(512)} %param.24) | copy-start | bytes 6148
Sparse Core Ops, SparseCore 0:
  9.9 82.9 all-gather.10
  94.8 43.7 all-gather.8
  141.2 73.7 all-gather.12
  307.9 85.3 all-gather.18
  395.8 79.0 all-gather.14
  477.2 79.8 all-gather.16
  565.0 47.7 reduce-scatter.1
where the time goes:
time: 622 us; the launch traced here: 620 us
  waiting for transfers between devices  440 us (71%)
  local copies, waits for them, and re-layouts  63.7 us (10%)
  matrix products  51.1 us (8%)
  blocking collectives  33.7 us (5%)
  other arithmetic  14.4 us (2%)
  between operations  13.7 us (2%)
    all_gather x1, waiting for transfers between devices, local(): lax.all_gather(w_value, 'context', axis=0, tiled=True)  81.4 us
    all_gather x1, waiting for transfers between devices, local(): lax.all_gather(w_gate, 'context', axis=0, tiled=True)  75.7 us
    all_gather x1, waiting for transfers between devices, local(): lax.all_gather(w_out, 'context', axis=1, tiled=True)  74 us
    all_gather x1, waiting for transfers between devices, local(): lax.all_gather(w_keys, 'context', axis=0, tiled=True)  68.9 us
    reduce_scatter x1, waiting for transfers between devices, local(): lax.psum_scatter(terms.astype(jnp.bfloat16), 'tensor', scatter_dimension=...  48 us
    all_gather x1, waiting for transfers between devices, local(): whole = lax.all_gather(tokens, 'tensor', axis=1, tiled=True)  45.6 us
    all_gather x1, waiting for transfers between devices, prefix(): lax.all_gather(a.astype(kind), axis)  40.9 us
    dynamic_update_slice x6, local copies, waits for them, and re-layouts, ssd_blocks(): final, outputs = lax.scan(fold, state, blocks)  38.5 us
  transfers between devices with their start and end apart: 8, of which 8 were waited for; matrix products, arithmetic and copies ran while one was open for 5% of the time, Pallas kernels for 0%

commit v1 on v0

v1 whole, which is shorter than its diff:
```python
import jax
import jax.numpy as jnp
from jax import lax
from jax.experimental import pallas as pl
from jax.experimental.pallas import tpu as pltpu
from jax.sharding import Mesh, PartitionSpec as P

F32 = jnp.float32
BF16 = jnp.bfloat16
HIGHEST = lax.Precision.HIGHEST

P_SIZE = 64
N = 128
TAPS = 4
HALO = 16
BLOCK = 128
VMEM = 48 * 1024 * 1024

CONTEXT = ("z", "y")
TENSOR = ("x", "core")


def params():
    return pltpu.CompilerParams(vmem_limit_bytes=VMEM)


def one_hot_heads(heads, width):
    head = lax.broadcasted_iota(jnp.int32, (heads, width), 0)
    column = lax.broadcasted_iota(jnp.int32, (heads, width), 1)
    return (column // P_SIZE == head).astype(F32)


def dot(a, b, contract=((1,), (0,)), precision=None):
    return lax.dot_general(a, b, (contract, ((), ())), precision=precision, preferred_element_type=F32)


def silu(v):
    return v / (1.0 + jnp.exp(-v))


def decays(step, rate, spread):
    rows = step.shape[0]
    r = lax.broadcasted_iota(jnp.int32, (rows, rows), 0)
    c = lax.broadcasted_iota(jnp.int32, (rows, rows), 1)
    run = dot((r >= c).astype(F32), -step * rate, precision=HIGHEST)
    last = run[rows - 1 : rows]
    mid = 0.5 * last
    grow = dot(jnp.exp(run - mid), spread, precision=HIGHEST)
    shrink = dot(step * jnp.exp(mid - run), spread, precision=HIGHEST)
    ends = dot(
        jnp.concatenate([jnp.exp(mid), jnp.exp(last - mid), jnp.exp(last), last] * 2, axis=0),
        spread,
        precision=HIGHEST,
    )
    return grow, shrink, ends


def raw_kernel(
    order, tok, wv, wk, taps_v, taps_k, step, rate, conv_out, state_out, total_out, acc
):
    turn = pl.program_id(0)
    value = wv.shape[1]

    @pl.when(turn == 0)
    def _():
        acc[...] = jnp.zeros_like(acc)

    acc[:, :value] += dot(tok[0], wv[...])
    acc[:, value:] += dot(tok[0], wk[...])

    @pl.when(turn == pl.num_programs(0) - 1)
    def _():
        heads = step.shape[1]
        spread = one_hot_heads(heads, value)
        acc[...] = acc[...].astype(BF16).astype(F32)
        taps = jnp.concatenate([taps_v[...], taps_k[...]], axis=1)
        state = jnp.zeros((N, value), F32)
        total = jnp.zeros((1, value), F32)
        for b in range(step.shape[0] // BLOCK):
            first = b * BLOCK
            summed = jnp.zeros((BLOCK, acc.shape[1]), F32)
            for tap in range(TAPS):
                start = HALO - (TAPS - 1) + first + tap
                summed = summed + taps[tap : tap + 1] * acc[start : start + BLOCK, :]
            convolved = silu(summed).astype(BF16)
            conv_out[first : first + BLOCK, :] = convolved
            _, shrink, ends = decays(step[first : first + BLOCK, :], rate[...], spread)
            signal = (convolved[:, :value].astype(F32) * shrink).astype(BF16)
            fresh = dot(convolved[:, value : value + N], signal, ((0,), (0,)))
            state = ends[2:3] * state + ends[1:2] * fresh
            total = total + ends[3:4]
        state_out[...] = state.astype(BF16)
        total_out[...] = jnp.broadcast_to(total, total_out.shape)


def prefix_kernel(states, out):
    pieces = states.shape[0]
    rows = out.shape[1]
    state = jnp.zeros((rows, out.shape[2]), F32)
    for piece in range(pieces):
        out[piece] = state.astype(BF16)
        block = states[piece].astype(F32)
        total = block[rows : rows + 1] + block[rows + 1 : rows + 2] + block[rows + 2 : rows + 3]
        state = jnp.exp(total) * state + block[:rows]


def scan_kernel(conv, step, rate, skip, start, out):
    value = out.shape[1]
    heads = step.shape[1]
    spread = one_hot_heads(heads, value)
    direct = dot(jnp.broadcast_to(skip[...], (8, heads)), spread, precision=HIGHEST)[0:1]
    r = lax.broadcasted_iota(jnp.int32, (BLOCK, BLOCK), 0)
    c = lax.broadcasted_iota(jnp.int32, (BLOCK, BLOCK), 1)
    state = start[...].astype(F32)
    for b in range(step.shape[0] // BLOCK):
        rows = slice(b * BLOCK, (b + 1) * BLOCK)
        grow, shrink, ends = decays(step[rows, :], rate[...], spread)
        signal = conv[rows, :value].astype(F32)
        write = conv[rows, value : value + N]
        read = conv[rows, value + N :]
        scores = jnp.where(r >= c, dot(read, write, ((1,), (1,))), 0.0).astype(BF16)
        scaled = (signal * shrink).astype(BF16)
        left = jnp.concatenate([scores, read], axis=1)
        right = jnp.concatenate([scaled, (state * ends[0:1]).astype(BF16)], axis=0)
        out[rows, :] = grow * dot(left, right) + direct * signal
        state = ends[2:3] * state + ends[1:2] * dot(write, scaled, ((0,), (0,)))


def gate_kernel(order, tok, wg, output, gain, normed, acc):
    turn = pl.program_id(0)

    @pl.when(turn == 0)
    def _():
        acc[...] = jnp.zeros_like(acc)

    acc[...] += dot(tok[0, HALO:, :], wg[...])

    @pl.when(turn == pl.num_programs(0) - 1)
    def _():
        gated = output[...] * silu(acc[...].astype(BF16).astype(F32))
        mean = jnp.mean(gated * gated, axis=1, keepdims=True)
        normed[...] = (gated * lax.rsqrt(mean + 1e-05) * gain[...]).astype(BF16)


def out_kernel(normed, w, out):
    out[...] = dot(normed[...], w[...], ((1,), (1,))).astype(BF16)


def local(
    tokens,
    w_gate,
    w_value,
    w_keys,
    conv_value,
    key_filter_taps,
    step,
    decay_rate,
    skip,
    norm_gain,
    w_out,
):
    rows, depth = tokens.shape
    value, keys = w_value.shape[1], w_keys.shape[1]
    heads = step.shape[1]
    pieces = lax.axis_size(CONTEXT)
    shares = lax.axis_size(TENSOR)
    rate = decay_rate[None, :]

    weights = lax.all_gather(
        jnp.concatenate([w_value, w_gate, w_out.T, w_keys], axis=1), CONTEXT, axis=0, tiled=True
    )
    route = [(i, i + 1) for i in range(pieces - 1)]
    before = lax.ppermute(tokens[rows - HALO :], CONTEXT, route)
    whole = lax.all_gather(jnp.concatenate([before, tokens], axis=0), TENSOR)
    order = jnp.zeros((8,), jnp.int32)

    convolved, own_state, total = pl.pallas_call(
        raw_kernel,
        grid_spec=pltpu.PrefetchScalarGridSpec(
            num_scalar_prefetch=1,
            grid=(shares,),
            in_specs=[
                pl.BlockSpec((1, rows + HALO, depth), lambda k, o: (k, 0, 0)),
                pl.BlockSpec((depth, value), lambda k, o: (k, 0)),
                pl.BlockSpec((depth, keys), lambda k, o: (k, 6)),
                pl.BlockSpec(conv_value.shape, lambda k, o: (0, 0)),
                pl.BlockSpec(key_filter_taps.shape, lambda k, o: (0, 0)),
                pl.BlockSpec(step.shape, lambda k, o: (0, 0)),
                pl.BlockSpec(rate.shape, lambda k, o: (0, 0)),
            ],
            out_specs=[
                pl.BlockSpec((rows, value + keys), lambda k, o: (0, 0)),
                pl.BlockSpec((N, value), lambda k, o: (0, 0)),
                pl.BlockSpec((8, value), lambda k, o: (0, 0)),
            ],
            scratch_shapes=[pltpu.VMEM((rows + HALO, value + keys), F32)],
        ),
        out_shape=[
            jax.ShapeDtypeStruct((rows, value + keys), BF16),
            jax.ShapeDtypeStruct((N, value), BF16),
            jax.ShapeDtypeStruct((8, value), F32),
        ],
        compiler_params=params(),
        name="raw",
    )(order, whole, weights, weights, conv_value, key_filter_taps, step, rate)

    slab = N // pieces
    high = total.astype(BF16)
    rest = total - high.astype(F32)
    middle = rest.astype(BF16)
    low = (rest - middle.astype(F32)).astype(BF16)
    totals = jnp.concatenate([high[:1], middle[:1], low[:1], jnp.zeros_like(low[:1])], axis=0)
    packed = jnp.concatenate(
        [own_state.reshape(pieces, slab, value), jnp.broadcast_to(totals, (pieces, 4, value))], axis=1
    )
    slices = lax.all_to_all(packed, CONTEXT, 0, 0, tiled=True)
    starts = pl.pallas_call(
        prefix_kernel,
        out_shape=jax.ShapeDtypeStruct((pieces, slab, value), BF16),
        compiler_params=params(),
        name="prefix",
    )(slices)
    start = lax.all_to_all(starts, CONTEXT, 0, 0, tiled=True).reshape(N, value)

    output = pl.pallas_call(
        scan_kernel,
        out_shape=jax.ShapeDtypeStruct((rows, value), F32),
        compiler_params=params(),
        name="scan",
    )(convolved, step, rate, skip[None, :], start)

    normed = pl.pallas_call(
        gate_kernel,
        grid_spec=pltpu.PrefetchScalarGridSpec(
            num_scalar_prefetch=1,
            grid=(shares,),
            in_specs=[
                pl.BlockSpec((1, rows + HALO, depth), lambda k, o: (k, 0, 0)),
                pl.BlockSpec((depth, value), lambda k, o: (k, 1)),
                pl.BlockSpec((rows, value), lambda k, o: (0, 0)),
                pl.BlockSpec((1, value), lambda k, o: (0, 0)),
            ],
            out_specs=pl.BlockSpec((rows, value), lambda k, o: (0, 0)),
            scratch_shapes=[pltpu.VMEM((rows, value), F32)],
        ),
        out_shape=jax.ShapeDtypeStruct((rows, value), BF16),
        compiler_params=params(),
        name="gate",
    )(order, whole, weights, output, norm_gain[None, :])

    terms = pl.pallas_call(
        out_kernel,
        grid=(shares,),
        in_specs=[
            pl.BlockSpec((rows, value), lambda j: (0, 0)),
            pl.BlockSpec((depth, value), lambda j: (j, 2)),
        ],
        out_specs=pl.BlockSpec((rows, depth), lambda j: (0, j)),
        out_shape=jax.ShapeDtypeStruct((rows, shares * depth), BF16),
        compiler_params=params(),
        name="out",
    )(normed, weights)
    return lax.psum_scatter(terms, TENSOR, scatter_dimension=1, tiled=True)


def solution(mesh):
    fine = Mesh(mesh.devices.reshape(8, 4, 4, 2), ("z", "y", "x", "core"))
    return jax.shard_map(
        local,
        mesh=fine,
        in_specs=(
            P(CONTEXT, TENSOR),
            P(CONTEXT, TENSOR),
            P(CONTEXT, TENSOR),
            P(CONTEXT, TENSOR),
            P(None, TENSOR),
            P(None, TENSOR),
            P(CONTEXT, TENSOR),
            P(TENSOR),
            P(TENSOR),
            P(TENSOR),
            P(TENSOR, CONTEXT),
        ),
        out_specs=P(CONTEXT, TENSOR),
        check_vma=False,
    )
```

time: 622 us -> 317 us (0.51)
  waiting for transfers between devices: 440 us -> 223 us
  local copies, waits for them, and re-layouts: 63.7 us -> 1.31 us
  matrix products: 51.1 us -> 0 us
  Pallas kernels: 0 us -> 40.7 us
  other arithmetic: 14.4 us -> 3.1 us
    all_gather x6 -> x2, waiting for transfers between devices: 387 us -> 180 us  [the longest x1 132 us: local(): lax.all_gather(jnp.concatenate([w_value, w_gate, w_out.T, w_keys], axis=1...]
    dot_general x17 -> x0, matrix products: 51.1 us -> none  [the longest x1 8.18 us: local(): jnp.dot(whole, lax.all_gather(w_gate, 'context', axis=0, tiled=True), pre...]
    pallas_call x0 -> x5, Pallas kernels: none -> 40.7 us  [the longest x1 15.7 us: local(): pl.pallas_call(raw_kernel, grid_spec=pltpu.PrefetchScalarGridSpec(num_sca...]
    dynamic_update_slice x6 -> x0, local copies, waits for them, and re-layouts: 38.5 us -> none  [ssd_blocks(): final, outputs = lax.scan(fold, state, blocks)]
    all_gather x1 -> x0, blocking collectives: 33.7 us -> none  [prefix(): lax.all_gather(a.astype(kind), axis)]
    all_to_all x0 -> x2, blocking collectives: none -> 30.1 us  [the longest x1 15.6 us: local(): slices = lax.all_to_all(packed, CONTEXT, 0, 0, tiled=True)]
    dynamic_slice x3 -> x0, local copies, waits for them, and re-layouts: 6.41 us -> none  [ssd_blocks(): final, outputs = lax.scan(fold, state, blocks)]
  transfers between devices with their start and end apart: 8 -> 4, of which waited for: 8 -> 4; matrix products, arithmetic and copies ran while one was open for 5% -> 0% of each run, Pallas kernels for 0% -> 0%
where the time goes in v1:
time: 317 us; the launch traced here: 316 us
  waiting for transfers between devices  223 us (70%)
  Pallas kernels  40.7 us (13%)
  blocking collectives  30.1 us (9%)
  between operations  13.3 us (4%)
  starting transfers between devices  4.13 us (1%)
    all_gather x1, waiting for transfers between devices, local(): lax.all_gather(jnp.concatenate([w_value, w_gate, w_out.T, w_keys], axis=1...  132 us
    all_gather x1, waiting for transfers between devices, local(): whole = lax.all_gather(jnp.concatenate([before, tokens], axis=0), TENSOR)  48.5 us
    reduce_scatter x1, waiting for transfers between devices, local(): return lax.psum_scatter(terms, TENSOR, scatter_dimension=1, tiled=True)  41.9 us
    pallas_call x1, Pallas kernels, local(): pl.pallas_call(raw_kernel, grid_spec=pltpu.PrefetchScalarGridSpec(num_sca...  15.7 us
    all_to_all x1, blocking collectives, local(): slices = lax.all_to_all(packed, CONTEXT, 0, 0, tiled=True)  15.6 us
    all_to_all x1, blocking collectives, local(): start = lax.all_to_all(starts, CONTEXT, 0, 0, tiled=True).reshape(N, value)  14.5 us
    pallas_call x1, Pallas kernels, local(): pl.pallas_call(gate_kernel, grid_spec=pltpu.PrefetchScalarGridSpec(num_sc...  9.72 us
    pallas_call x1, Pallas kernels, local(): pl.pallas_call(out_kernel, grid=(shares,), in_specs=[pl.BlockSpec((rows,...  9.18 us
  transfers between devices with their start and end apart: 4, of which 4 were waited for; matrix products, arithmetic and copies ran while one was open for 0% of the time, Pallas kernels for 0%

profile of v1, /device:TPU:1, one launch (start us, length us, event | category | flops | bytes accessed | tf_op | source)
XLA Modules:
  0.0 315.9 jit_solution(650796535555770198)
XLA Ops:
  6.5 0.0 all-gather.6.cloned.1.call-start
  6.6 0.8 slice.12
  7.4 4.0 %collective-permute-start = (bf16[16,512]{1,0:T(8,128)(2,1)S(1)}, bf16[16,512]{1,0:T(8,128)(2,1)S(1)}, u32[]{:S(2)}, u32[]{:S(2)}) collective-permute-start(bf16[16,512]{1,0:T(8,128)(2,1)S(1)} %slice.12), channel_id=1, source_target_pairs={{0,8},{8,16},{16,24},{24,32},{32,40},{40,48},{48,56},{56,64},{64,7... | collective-permute-start | bytes 49160 | tf_op jit(solution)/shard_map/ppermute | solution.py:173
  11.4 0.9 collective-permute-done
  12.3 2.1 pad_maximum_fusion
  14.3 0.0 all-gather.6.cloned.1.call-update
  14.4 0.0 all-gather.4.cloned.1.call-start
  14.4 0.0 copy-done.7
  14.4 0.1 copy.12
  14.6 0.0 copy-done.8
  14.6 0.8 pad_maximum_fusion.1
  15.4 0.0 all-gather.4.cloned.1.call-update
  15.4 0.0 reduce-scatter.2.cloned.1.call-start
  15.5 0.2 copy.13.step
  15.6 0.1 pad.5.clone
  15.7 48.5 %all-gather.6.cloned.1.call-done = bf16[6272,512]{1,0:T(8,128)(2,1)} async-done(((bf16[784,512]{1,0:T(8,128)(2,1)}), bf16[6272,512]{1,0:T(8,128)(2,1)}) %all-gather.6.cloned.1.call-update) | async-done | bytes 6422544 | tf_op jit(solution)/shard_map/all_gather | solution.py:174
  64.2 132.0 %all-gather.4.cloned.1.call-done.wv.wk.wg.w = bf16[4096,1792]{1,0:T(8,128)(2,1)} async-done(((bf16[128,1792]{1,0:T(8,128)(2,1)}), bf16[4096,1792]{1,0:T(8,128)(2,1)}) %all-gather.4.cloned.1.call-update) | async-done | bytes 14680080 | tf_op jit(solution)/shard_map/all_gather | solution.py:169
  196.2 0.0 copy-done.1
  196.2 15.7 %raw.1 = (bf16[768,768]{1,0:T(8,128)(2,1)S(1)}, bf16[128,512]{1,0:T(8,128)(2,1)S(1)}, f32[8,512]{1,0:T(8,128)S(1)}) custom-call(s32[8]{0:T(128)S(1)} %broadcast_1_order.2.order, bf16[8,784,512]{2,1,0:T(8,128)(2,1)} %bitcast.10, bf16[4096,1792]{1,0:T(8,128)(2,1)} %all-gather.4.cloned.1.call-done.wv.wk.wg.w, ...), custom_call_target="tpu_custom_call" | custom-call | tf_op jit(solution)/shard_map/raw/pallas_call | solution.py:177
  211.9 0.0 copy-start.4
  212.0 0.1 maximum_maximum_fusion
  212.1 0.1 pad_maximum_fusion.2
  212.3 15.6 %all_to_all.10.states = bf16[32,8,512]{2,1,0:T(8,128)(2,1)S(1)} all-to-all(bf16[32,8,512]{2,1,0:T(8,128)(2,1)S(1)} %pad_maximum_fusion.2), channel_id=1, replica_groups=mesh['z'=8,'y'=4,'x'=4,'core'=2] {'z','y'}, dimensions={0} | all-to-all | bytes 524288 | tf_op jit(solution)/shard_map/all_to_all | solution.py:216
  227.8 0.2 prefix.1
  228.0 14.5 %all_to_all.11 = bf16[32,4,512]{2,1,0:T(4,128)(2,1)S(1)} all-to-all(bf16[32,4,512]{2,1,0:T(4,128)(2,1)S(1)} %prefix.1), channel_id=1, replica_groups=mesh['z'=8,'y'=4,'x'=4,'core'=2] {'z','y'}, dimensions={0} | all-to-all | bytes 262144 | tf_op jit(solution)/shard_map/all_to_all | solution.py:223
  242.6 0.0 copy-done.4
  242.6 0.0 copy-start.3
  242.6 5.8 %scan.1.output = f32[768,512]{1,0:T(8,128)S(1)} custom-call(bf16[768,768]{1,0:T(8,128)(2,1)S(1)} %get-tuple-element.8.conv, f32[768,8]{1,0:T(8,128)S(1)} %copy.13.step, f32[1,8]{1,0:T(1,128)S(1)} %bitcast.7, f32[1,8]{1,0:T(1,128)S(1)} %bitcast.9, bf16[128,512]{1,0:T(8,128)(2,1)S(1)} %reshape.7.start), custom_call_target="tpu_custom_call" | custom-call | tf_op jit(solution)/shard_map/scan/pallas_call | solution.py:225
  248.5 9.7 %gate.1.normed = bf16[768,512]{1,0:T(8,128)(2,1)S(1)} custom-call(s32[8]{0:T(128)S(1)} %broadcast_1_order.2.order, bf16[8,784,512]{2,1,0:T(8,128)(2,1)} %bitcast.11, bf16[4096,1792]{1,0:T(8,128)(2,1)} %all-gather.4.cloned.1.call-done.wv.wk.wg.w, f32[768,512]{1,0:T(8,128)S(1)} %scan.1.output, f32[1,512]{1,0:T(1,128)S(1)} %bitcast.8), custom_call_target="tpu_custom_call" | custom-call | tf_op jit(solution)/shard_map/gate/pallas_call | solution.py:232
  258.2 9.2 %out.1 = bf16[768,4096]{1,0:T(8,128)(2,1)} custom-call(bf16[768,512]{1,0:T(8,128)(2,1)S(1)} %gate.1.normed, bf16[4096,1792]{1,0:T(8,128)(2,1)} %all-gather.4.cloned.1.call-done.wv.wk.wg.w), custom_call_target="tpu_custom_call" | custom-call | tf_op jit(solution)/shard_map/out/pallas_call | solution.py:251
  267.4 0.0 reduce-scatter.2.cloned.1.call-update
  267.4 41.9 %reduce-scatter.2.cloned.1.call-done = bf16[768,512]{1,0:T(8,128)(2,1)} async-done(((bf16[768,4096]{1,0:T(8,128)(2,1)}), bf16[768,512]{1,0:T(8,128)(2,1)}) %reduce-scatter.2.cloned.1.call-update) | async-done | bytes 786448 | tf_op jit(solution)/shard_map/reduce_scatter | solution.py:263
  (22 shorter events, 0.2 us)
Async XLA Ops:
  6.5 7.9 %copy-start.7 = (bf16[512,128]{1,0:T(8,128)(2,1)S(1)}, bf16[512,128]{1,0:T(8,128)(2,1)}, u32[]{:S(2)}) copy-start(bf16[512,128]{1,0:T(8,128)(2,1)} %param.21) | copy-start | bytes 393220
  6.5 8.0 %copy-start.8 = (bf16[128,256]{1,0:T(8,128)(2,1)S(1)}, bf16[128,256]{1,0:T(8,128)(2,1)}, u32[]{:S(2)}) copy-start(bf16[128,256]{1,0:T(8,128)(2,1)} %param.14) | copy-start | bytes 196612
  6.5 8.0 %copy-start.6 = (bf16[128,512]{1,0:T(8,128)(2,1)S(1)}, bf16[128,512]{1,0:T(8,128)(2,1)}, u32[]{:S(2)}) copy-start(bf16[128,512]{1,0:T(8,128)(2,1)} %param.13) | copy-start | bytes 393220
  6.5 8.0 %copy-start.5 = (bf16[128,512]{1,0:T(8,128)(2,1)S(1)}, bf16[128,512]{1,0:T(8,128)(2,1)}, u32[]{:S(2)}) copy-start(bf16[128,512]{1,0:T(8,128)(2,1)} %param.12) | copy-start | bytes 393220
  6.5 57.6 %all-gather.6.cloned.1.call-start = ((), (), s32[]{:S(2)}) async-start(), calls=%async_computation.5 | async-start | bytes 7225344 | tf_op jit(solution)/shard_map/all_gather | solution.py:174
  7.4 4.9 %collective-permute-start = (bf16[16,512]{1,0:T(8,128)(2,1)S(1)}, bf16[16,512]{1,0:T(8,128)(2,1)S(1)}, u32[]{:S(2)}, u32[]{:S(2)}) collective-permute-start(bf16[16,512]{1,0:T(8,128)(2,1)S(1)} %slice.12), channel_id=1, source_target_pairs={{0,8},{8,16},{16,24},{24,32},{32,40},{40,48},{48,56},{56,64},{64,7... | collective-permute-start | bytes 49160 | tf_op jit(solution)/shard_map/ppermute | solution.py:173
  14.3 1.1 copy-start.9
  14.3 181.8 %copy-start = (f32[4,512]{1,0:T(4,128)S(1)}, f32[4,512]{1,0:T(4,128)}, u32[]{:S(2)}) copy-start(f32[4,512]{1,0:T(4,128)} %taps_v.1) | copy-start | bytes 24580
  14.3 181.8 %copy-start.1 = (f32[4,256]{1,0:T(4,128)S(1)}, f32[4,256]{1,0:T(4,128)}, u32[]{:S(2)}) copy-start(f32[4,256]{1,0:T(4,128)} %taps_k.1) | copy-start | bytes 12292
  14.3 181.8 %copy-start.2 = (f32[8]{0:T(128)S(1)}, f32[8]{0:T(128)}, u32[]{:S(2)}) copy-start(f32[8]{0:T(128)} %param.18) | copy-start | bytes 100
  14.4 181.8 %all-gather.4.cloned.1.call-start = ((), (), s32[]{:S(2)}) async-start(), calls=%async_computation.3 | async-start | bytes 15138816 | tf_op jit(solution)/shard_map/all_gather | solution.py:169
  15.4 293.9 %reduce-scatter.2.cloned.1.call-start = ((), (), s32[]{:S(2)}) async-start(), calls=%async_computation.4 | async-start | bytes 7077888 | tf_op jit(solution)/shard_map/reduce_scatter | solution.py:263
  211.9 30.7 %copy-start.4 = (f32[8]{0:T(128)S(1)}, f32[8]{0:T(128)}, u32[]{:S(2)}) copy-start(f32[8]{0:T(128)} %param.19) | copy-start | bytes 100
  242.6 5.9 %copy-start.3 = (f32[512]{0:T(512)S(1)}, f32[512]{0:T(512)}, u32[]{:S(2)}) copy-start(f32[512]{0:T(512)} %param.20) | copy-start | bytes 6148
Sparse Core Ops, SparseCore 0:
  14.5 49.6 all-gather.5
  66.7 129.3 all-gather.3
  267.5 41.7 reduce-scatter.1

commit v2 on v1

v2 whole, which is shorter than its diff:
```python
import jax
import jax.numpy as jnp
from jax import lax
from jax.experimental import pallas as pl
from jax.experimental.pallas import tpu as pltpu
from jax.sharding import Mesh, PartitionSpec as P

F32 = jnp.float32
BF16 = jnp.bfloat16
HIGHEST = lax.Precision.HIGHEST

P_SIZE = 64
N = 128
TAPS = 4
HALO = 16
BLOCK = 128
CONTEXT = ("z", "y")
TENSOR = ("x", "core")


def params(mebibytes):
    return pltpu.CompilerParams(vmem_limit_bytes=mebibytes * 1024 * 1024)


def cost(flops, bytes_accessed):
    return pl.CostEstimate(flops=flops, bytes_accessed=bytes_accessed, transcendentals=0)


def one_hot_heads(heads, width):
    head = lax.broadcasted_iota(jnp.int32, (heads, width), 0)
    column = lax.broadcasted_iota(jnp.int32, (heads, width), 1)
    return (column // P_SIZE == head).astype(F32)


def dot(a, b, contract=((1,), (0,)), precision=None):
    return lax.dot_general(a, b, (contract, ((), ())), precision=precision, preferred_element_type=F32)


def silu(v):
    return v / (1.0 + jnp.exp(-v))


def decays(step, rate, spread):
    rows = step.shape[0]
    r = lax.broadcasted_iota(jnp.int32, (rows, rows), 0)
    c = lax.broadcasted_iota(jnp.int32, (rows, rows), 1)
    run = dot((r >= c).astype(F32), -step * rate, precision=HIGHEST)
    last = run[rows - 1 : rows]
    mid = 0.5 * last
    grow = dot(jnp.exp(run - mid), spread, precision=HIGHEST)
    shrink = dot(step * jnp.exp(mid - run), spread, precision=HIGHEST)
    ends = dot(
        jnp.concatenate([jnp.exp(mid), jnp.exp(last - mid), jnp.exp(last), last] * 2, axis=0),
        spread,
        precision=HIGHEST,
    )
    return grow, shrink, ends


def block_of(place, piece):
    x, core = place[2], place[3]
    other = piece // 4
    return lax.rem(x + piece % 4, 4) * 2 + (core if other == 0 else 1 - core)


def start_rows(block, y, quarters, target, sems):
    here, ahead, across, across_rest, behind = quarters
    rows = here.shape[1]

    def start(d, source, index):
        at = pl.ds(pl.multiple_of(lax.rem(y + d, 4) * rows, rows), rows)
        pltpu.make_async_copy(source.at[index], target.at[at], sems.at[d]).start()

    start(0, here, block)
    start(1, ahead, block)
    start(3, behind, block)
    half = across.shape[0]

    @pl.when(block < half)
    def _():
        start(2, across, block)

    @pl.when(block >= half)
    def _():
        start(2, across_rest, block - half)


def wait_rows(source, target, sems):
    rows = source.shape[1]
    for d in range(4):
        at = pl.ds(d * rows, rows)
        pltpu.make_async_copy(source.at[0], target.at[at], sems.at[d]).wait()


def raw_kernel(place, *refs):
    pieces, refs = refs[:8], refs[8:]
    halo, values, refs = refs[0], refs[1:6], refs[6:]
    keys, taps_v, taps_k, step, rate, *refs = refs
    conv_out, packed_out, tok, wv, wk, acc, tok_sems, halo_sems, v_sems, k_sems = refs
    rows, depth = pieces[0].shape
    value = taps_v.shape[1]
    for i in range(8):
        pltpu.make_async_copy(pieces[i], tok.at[i, pl.ds(HALO, rows)], tok_sems.at[i]).start()
        pltpu.make_async_copy(halo.at[i], tok.at[i, pl.ds(0, HALO)], halo_sems.at[i]).start()
        block = block_of(place, i)
        start_rows(block, place[1], values, wv.at[i], v_sems.at[i])
        at = pl.ds(pl.multiple_of(block * depth, depth), depth)
        pltpu.make_async_copy(keys.at[at], wk.at[i], k_sems.at[i]).start()

    acc[...] = jnp.zeros_like(acc)

    def turn(i, carry):
        pltpu.make_async_copy(pieces[0], tok.at[i, pl.ds(HALO, rows)], tok_sems.at[i]).wait()
        pltpu.make_async_copy(halo.at[i], tok.at[i, pl.ds(0, HALO)], halo_sems.at[i]).wait()
        wait_rows(values[0], wv.at[i], v_sems.at[i])
        pltpu.make_async_copy(keys.at[pl.ds(0, depth)], wk.at[i], k_sems.at[i]).wait()
        acc[:, :value] += dot(tok[i], wv[i])
        acc[:, value:] += dot(tok[i], wk[i])
        return carry

    lax.fori_loop(0, 8, turn, 0)

    heads = step.shape[1]
    spread = one_hot_heads(heads, value)
    acc[...] = acc[...].astype(BF16).astype(F32)
    taps = jnp.concatenate([taps_v[...], taps_k[...]], axis=1)
    state = jnp.zeros((N, value), F32)
    total = jnp.zeros((1, value), F32)
    for b in range(step.shape[0] // BLOCK):
        first = b * BLOCK
        summed = jnp.zeros((BLOCK, acc.shape[1]), F32)
        for tap in range(TAPS):
            start = HALO - (TAPS - 1) + first + tap
            summed = summed + taps[tap : tap + 1] * acc[start : start + BLOCK, :]
        convolved = silu(summed).astype(BF16)
        conv_out[first : first + BLOCK, :] = convolved
        _, shrink, ends = decays(step[first : first + BLOCK, :], rate[...], spread)
        signal = (convolved[:, :value].astype(F32) * shrink).astype(BF16)
        fresh = dot(convolved[:, value : value + N], signal, ((0,), (0,)))
        state = ends[2:3] * state + ends[1:2] * fresh
        total = total + ends[3:4]
    high = total.astype(BF16).astype(F32)
    middle = (total - high).astype(BF16).astype(F32)
    low = total - high - middle
    totals = jnp.concatenate([high, middle, low, jnp.zeros_like(low)], axis=0)
    for p in range(packed_out.shape[0]):
        slab = N // packed_out.shape[0]
        packed_out[p] = jnp.concatenate([state[p * slab : (p + 1) * slab], totals], axis=0).astype(BF16)


def prefix_kernel(states, earlier, out):
    pieces = states.shape[0]
    rows = out.shape[1]
    state = jnp.zeros((rows, out.shape[2]), F32)
    for piece in range(pieces):
        out[piece] = state.astype(BF16)
        block = states[piece].astype(F32)
        total = block[rows : rows + 1] + block[rows + 1 : rows + 2] + block[rows + 2 : rows + 3]
        state = jnp.exp(total) * state + block[:rows]


def scan_kernel(conv, step, rate, skip, out):
    value = out.shape[1]
    heads = step.shape[1]
    spread = one_hot_heads(heads, value)
    direct = dot(jnp.broadcast_to(skip[...], (8, heads)), spread, precision=HIGHEST)[0:1]
    r = lax.broadcasted_iota(jnp.int32, (BLOCK, BLOCK), 0)
    c = lax.broadcasted_iota(jnp.int32, (BLOCK, BLOCK), 1)
    state = jnp.zeros((N, value), F32)
    for b in range(step.shape[0] // BLOCK):
        rows = slice(b * BLOCK, (b + 1) * BLOCK)
        grow, shrink, ends = decays(step[rows, :], rate[...], spread)
        signal = conv[rows, :value].astype(F32)
        write = conv[rows, value : value + N]
        read = conv[rows, value + N :]
        scores = jnp.where(r >= c, dot(read, write, ((1,), (1,))), 0.0).astype(BF16)
        scaled = (signal * shrink).astype(BF16)
        left = jnp.concatenate([scores, read], axis=1)
        right = jnp.concatenate([scaled, (state * ends[0:1]).astype(BF16)], axis=0)
        out[rows, :] = grow * dot(left, right) + direct * signal
        state = ends[2:3] * state + ends[1:2] * dot(write, scaled, ((0,), (0,)))


def gate_kernel(place, *refs):
    pieces, refs = refs[:8], refs[8:]
    gates, refs = refs[:5], refs[5:]
    out, tok, wg, acc, tok_sems, w_sems = refs
    for i in range(8):
        pltpu.make_async_copy(pieces[i], tok.at[i], tok_sems.at[i]).start()
        start_rows(block_of(place, i), place[1], gates, wg.at[i], w_sems.at[i])

    acc[...] = jnp.zeros_like(acc)

    def turn(i, carry):
        pltpu.make_async_copy(pieces[0], tok.at[i], tok_sems.at[i]).wait()
        wait_rows(gates[0], wg.at[i], w_sems.at[i])
        acc[...] += dot(tok[i], wg[i])
        return carry

    lax.fori_loop(0, 8, turn, 0)
    out[...] = acc[...].astype(BF16)


def norm_kernel(output, conv, step, rate, start, gate, gain, normed):
    value = output.shape[1]
    spread = one_hot_heads(step.shape[1], value)
    r = lax.broadcasted_iota(jnp.int32, (BLOCK, BLOCK), 0)
    c = lax.broadcasted_iota(jnp.int32, (BLOCK, BLOCK), 1)
    lower = (r >= c).astype(F32)
    so_far = jnp.zeros((1, step.shape[1]), F32)
    before = [start[p].astype(F32) for p in range(start.shape[0])]
    before = jnp.concatenate(before, axis=0).astype(BF16)
    for b in range(step.shape[0] // BLOCK):
        rows = slice(b * BLOCK, (b + 1) * BLOCK)
        run = so_far + dot(lower, -step[rows, :] * rate[...], precision=HIGHEST)
        so_far = run[BLOCK - 1 :]
        kept = dot(jnp.exp(run), spread, precision=HIGHEST)
        total = output[rows, :] + kept * dot(conv[rows, value + N :], before)
        gated = total * silu(gate[rows, :].astype(F32))
        mean = jnp.mean(gated * gated, axis=1, keepdims=True)
        normed[rows, :] = (gated * lax.rsqrt(mean + 1e-05) * gain[...]).astype(BF16)


def out_kernel(targets, own, sibling, w_own, w_sibling, earlier, *outs):
    term = dot(own[...], w_own[...], ((1,), (1,))) + dot(sibling[...], w_sibling[...], ((1,), (1,)))
    for job, out in enumerate(outs):

        @pl.when(pl.program_id(0) == job)
        def _():
            out[...] = term.astype(out.dtype)


def shifted(array, axis, distance):
    size = lax.axis_size(axis)
    return lax.ppermute(array, axis, [((i + distance) % size, i) for i in range(size)])


def quad(array):
    near = jnp.concatenate([array] + [shifted(array, "y", d) for d in (1, 2, 3)], axis=0)
    return jnp.roll(near, lax.axis_index("y") * array.shape[0], axis=0)


def after(array, *others):
    return lax.optimization_barrier((array, *others))[0]


def local(
    tokens,
    w_gate,
    w_value,
    w_keys,
    conv_value,
    key_filter_taps,
    step,
    decay_rate,
    skip,
    norm_gain,
    w_out,
):
    rows, depth = tokens.shape
    value, keys = w_value.shape[1], w_keys.shape[1]
    heads = step.shape[1]
    pieces = lax.axis_size(CONTEXT)
    shares = lax.axis_size(TENSOR)
    rate = decay_rate[None, :]

    both = lax.all_gather(jnp.concatenate([w_value, w_gate], axis=1), "z")
    keys_four = quad(w_keys)
    swap = []
    for z in range(8):
        for c in range(2):
            swap.append((2 * z + c, 2 * z + c if z % 2 == c else 2 * (z ^ 1) + 1 - c))
    turned = lax.ppermute(after(w_out, keys_four).T, ("z", "core"), swap)
    outs_four = quad(turned)
    ahead, behind = shifted(tokens, "x", 1), shifted(tokens, "x", -1)
    across = shifted(ahead, "x", 1)
    keys_all = lax.all_gather(keys_four, "z", axis=0, tiled=True)
    both, ahead, behind, across, outs_four = after((both, ahead, behind, across, outs_four))
    v0, g0 = both[..., :value], both[..., value:]
    v1, v3 = shifted(v0, "y", 1), shifted(v0, "y", -1)
    own_all = [tokens, ahead, across, behind]
    all_tokens = own_all + [shifted(after(a, both), "core", 1) for a in own_all]
    route = [(i, i + 1) for i in range(pieces - 1)]
    halo = lax.ppermute(jnp.stack([a[rows - HALO :] for a in all_tokens]), CONTEXT, route)
    outs = lax.all_gather(outs_four, "z", axis=0, tiled=True)
    v1, v3, halo, *all_tokens = after((v1, v3, halo, *all_tokens))
    v2 = shifted(v1[:4], "y", 1), shifted(v3[4:], "y", -1)
    g0 = after(g0, *v2)
    g1, g3 = shifted(g0, "y", 1), shifted(g0, "y", -1)
    place = jnp.stack([lax.axis_index(a) for a in ("z", "y", "x", "core")]).astype(jnp.int32)

    anywhere = pl.BlockSpec(memory_space=pl.ANY)
    smem = pl.BlockSpec(memory_space=pltpu.SMEM)
    vmem = pl.BlockSpec(memory_space=pltpu.VMEM)
    convolved, packed = pl.pallas_call(
        raw_kernel,
        in_specs=[smem] + [anywhere] * 15 + [vmem] * 4,
        out_specs=[vmem] * 2,
        scratch_shapes=[
            pltpu.VMEM((8, rows + HALO, depth), BF16),
            pltpu.VMEM((8, depth, value), BF16),
            pltpu.VMEM((8, depth, keys), BF16),
            pltpu.VMEM((rows + HALO, value + keys), F32),
            pltpu.SemaphoreType.DMA((8,)),
            pltpu.SemaphoreType.DMA((8,)),
            pltpu.SemaphoreType.DMA((8, 4)),
            pltpu.SemaphoreType.DMA((8,)),
        ],
        out_shape=[
            jax.ShapeDtypeStruct((rows, value + keys), BF16),
            jax.ShapeDtypeStruct((pieces, N // pieces + 4, value), BF16),
        ],
        compiler_params=params(58),
        name="raw",
    )(
        place, *all_tokens, halo, v0, v1, *v2, v3, keys_all,
        conv_value, key_filter_taps, step, rate,
    )

    slices = lax.all_to_all(packed, CONTEXT, 0, 0, tiled=True)
    g1, g3, _ = after((g1, g3, packed))
    g2 = shifted(g1[:4], "y", 1), shifted(g3[4:], "y", -1)
    output = pl.pallas_call(
        scan_kernel,
        out_shape=jax.ShapeDtypeStruct((rows, value), F32),
        compiler_params=params(58),
        name="scan",
    )(convolved, step, rate, skip[None, :])

    starts = pl.pallas_call(
        prefix_kernel,
        in_specs=[vmem, anywhere],
        out_specs=vmem,
        out_shape=jax.ShapeDtypeStruct((pieces, N // pieces, value), BF16),
        compiler_params=params(58),
        name="prefix",
    )(slices, output)
    start = lax.all_to_all(starts, CONTEXT, 0, 0, tiled=True)

    gate = pl.pallas_call(
        gate_kernel,
        in_specs=[smem] + [anywhere] * 13,
        out_specs=vmem,
        scratch_shapes=[
            pltpu.VMEM((8, rows, depth), BF16),
            pltpu.VMEM((8, depth, value), BF16),
            pltpu.VMEM((rows, value), F32),
            pltpu.SemaphoreType.DMA((8,)),
            pltpu.SemaphoreType.DMA((8, 4)),
        ],
        out_shape=jax.ShapeDtypeStruct((rows, value), BF16),
        compiler_params=params(58),
        name="gate",
    )(place, *all_tokens, g0, g1, *g2, g3)

    normed = pl.pallas_call(
        norm_kernel,
        out_shape=jax.ShapeDtypeStruct((rows, value), BF16),
        compiler_params=params(58),
        name="norm",
    )(output, convolved, step, rate, start, gate, norm_gain[None, :])

    x, core = lax.axis_index("x"), lax.axis_index("core")

    half = rows // 2
    sibling = shifted(normed, "core", 1)

    def terms(earlier, *jobs):
        count = len(jobs)
        goals = [(x + d) % 4 * 2 + c for c in (core, 1 - core) for d, _, _ in jobs]
        goals = jnp.stack(goals + [part for _, part, _ in jobs]).astype(jnp.int32)
        part = pl.BlockSpec((half, value), lambda j, t: (t[2 * count + j], 0))
        return pl.pallas_call(
            out_kernel,
            grid_spec=pltpu.PrefetchScalarGridSpec(
                num_scalar_prefetch=1,
                grid=(count,),
                in_specs=[
                    part,
                    part,
                    pl.BlockSpec((depth, value), lambda j, t: (t[j], 0)),
                    pl.BlockSpec((depth, value), lambda j, t: (t[count + j], 0)),
                    anywhere,
                ],
                out_specs=[pl.BlockSpec((half, depth), lambda j, t: (0, 0))] * count,
            ),
            out_shape=[jax.ShapeDtypeStruct((half, depth), kind) for _, _, kind in jobs],
            compiler_params=params(58),
            cost_estimate=cost(4 * count * half * depth * value, 2 * count * depth * value),
            name="out",
        )(goals, normed, sibling, outs, outs, earlier)

    far_upper, far_lower = terms(normed, (2, 0, BF16), (2, 1, BF16))
    from_behind = shifted(far_upper, "x", -1)
    from_ahead = shifted(far_lower, "x", 1)
    lower_ahead, upper_behind, upper_ahead, lower_behind = terms(
        far_upper, (1, 1, BF16), (3, 0, BF16), (1, 0, F32), (3, 1, F32)
    )
    lower = shifted(lower_ahead, "x", -1)
    upper = shifted(upper_behind, "x", 1)
    upper_ahead = (upper_ahead + from_behind.astype(F32)).astype(BF16)
    lower_behind = (lower_behind + from_ahead.astype(F32)).astype(BF16)
    here_upper, here_lower = terms(upper_ahead, (0, 0, F32), (0, 1, F32))
    upper = here_upper + upper.astype(F32) + shifted(upper_ahead, "x", -1).astype(F32)
    lower = here_lower + lower.astype(F32) + shifted(lower_behind, "x", 1).astype(F32)
    return jnp.concatenate([upper, lower], axis=0).astype(BF16)


def solution(mesh):
    fine = Mesh(mesh.devices.reshape(8, 4, 4, 2), ("z", "y", "x", "core"))
    return jax.shard_map(
        local,
        mesh=fine,
        in_specs=(
            P(CONTEXT, TENSOR),
            P(CONTEXT, TENSOR),
            P(CONTEXT, TENSOR),
            P(CONTEXT, TENSOR),
            P(None, TENSOR),
            P(None, TENSOR),
            P(CONTEXT, TENSOR),
            P(TENSOR),
            P(TENSOR),
            P(TENSOR),
            P(TENSOR, CONTEXT),
        ),
        out_specs=P(CONTEXT, TENSOR),
        check_vma=False,
    )
```

time: 317 us -> 244 us (0.77)
  the two profiles are of different devices: /device:TPU:1 before, /device:TPU:14 now
where the time goes in v2:
time: 244 us; the launch traced here: 240 us
  waiting for transfers between devices  76.8 us (31%)
  starting transfers between devices  69.1 us (28%)
  Pallas kernels  58.6 us (24%)
  local copies, waits for them, and re-layouts  15.9 us (7%)
  between operations  13.8 us (6%)
  other arithmetic  6.12 us (3%)
    ppermute x28, waiting for transfers between devices, shifted(): lax.ppermute(array, axis, [((i + distance) % size, i) for i in range(size)])  57.2 us
    ppermute x28, starting transfers between devices, shifted(): lax.ppermute(array, axis, [((i + distance) % size, i) for i in range(size)])  41.8 us
    ppermute x1, waiting for transfers between devices, local(): lax.ppermute(jnp.stack([a[rows - HALO:] for a in all_tokens]), CONTEXT, r...  19.5 us
    pallas_call x1, Pallas kernels, local(): pl.pallas_call(raw_kernel, in_specs=[smem] + [anywhere] * 15 + [vmem] * 4...  17.1 us
    pallas_call x3, Pallas kernels, terms(): pl.pallas_call(out_kernel, grid_spec=pltpu.PrefetchScalarGridSpec(num_sca...  16.2 us
    all_to_all x1, starting transfers between devices, local(): slices = lax.all_to_all(packed, CONTEXT, 0, 0, tiled=True)  12 us
    all_to_all x1, starting transfers between devices, local(): start = lax.all_to_all(starts, CONTEXT, 0, 0, tiled=True)  10.7 us
    pallas_call x1, Pallas kernels, local(): pl.pallas_call(gate_kernel, in_specs=[smem] + [anywhere] * 13, out_specs=...  8.93 us
  transfers between devices with their start and end apart: 35, of which 15 were waited for; matrix products, arithmetic and copies ran while one was open for 6% of the time, Pallas kernels for 23%

profile of v2, /device:TPU:14, one launch (start us, length us, event | category | flops | bytes accessed | tf_op | source)
XLA Modules:
  0.0 240.2 jit_solution(5682830955957932603)
XLA Ops:
  6.5 1.8 pad_maximum_fusion.1
  8.9 2.6 %collective-permute-start.4 = (bf16[128,256]{1,0:T(8,128)(2,1)}, bf16[128,256]{1,0:T(8,128)(2,1)S(1)}, u32[]{:S(2)}, u32[]{:S(2)}) collective-permute-start(bf16[128,256]{1,0:T(8,128)(2,1)} %param.14), channel_id=1, source_target_pairs={{16,0},{24,8},{0,16},{8,24},{17,1},{25,9},{1,17},{9,25},{18,2},{26... | collective-permute-start | bytes 196616 | tf_op jit(solution)/shard_map/ppermute | solution.py:235
  11.5 1.9 collective-permute-start.5
  19.4 2.7 %collective-permute-start.7 = (bf16[128,512]{1,0:T(8,128)(2,1)S(1)}, bf16[128,512]{1,0:T(8,128)(2,1)S(1)}, u32[]{:S(2)}, u32[]{:S(2)}) collective-permute-start(bf16[128,512]{1,0:T(8,128)(2,1)S(1)} %collective-permute-done.6), channel_id=1, source_target_pairs={{8,0},{16,8},{24,16},{0,24},{9,1},{17,9},{25,17},{1,25},{10,2},{18... | collective-permute-start | bytes 393224 | tf_op jit(solution)/shard_map/ppermute | solution.py:235
  22.1 2.4 %collective-permute-start.1 = (bf16[768,512]{1,0:T(8,128)(2,1)S(1)}, bf16[768,512]{1,0:T(8,128)(2,1)S(1)}, u32[]{:S(2)}, u32[]{:S(2)}) collective-permute-start(bf16[768,512]{1,0:T(8,128)(2,1)S(1)} %copy-done.3), channel_id=1, source_target_pairs={{6,0},{0,2},{2,4},{4,6},{7,1},{1,3},{3,5},{5,7},{14,8},{8,10},{10,... | collective-permute-start | bytes 2359304 | tf_op jit(solution)/shard_map/ppermute | solution.py:235
  26.6 10.4 %collective-permute-done.refs_1_ = bf16[768,512]{1,0:T(8,128)(2,1)S(1)} collective-permute-done((bf16[768,512]{1,0:T(8,128)(2,1)S(1)}, bf16[768,512]{1,0:T(8,128)(2,1)S(1)}, u32[]{:S(2)}, u32[]{:S(2)}) %collective-permute-start) | collective-permute-done | bytes 786464 | tf_op jit(solution)/shard_map/ppermute | solution.py:235
  38.2 17.5 %collective-permute-done.2.refs_2_ = bf16[768,512]{1,0:T(8,128)(2,1)} collective-permute-done((bf16[768,512]{1,0:T(8,128)(2,1)S(1)}, bf16[768,512]{1,0:T(8,128)(2,1)}, u32[]{:S(2)}, u32[]{:S(2)}) %collective-permute-start.2) | collective-permute-done | bytes 786464 | tf_op jit(solution)/shard_map/ppermute | solution.py:235
  55.9 1.9 fusion
  57.8 2.2 collective-permute-start.10
  64.7 3.8 %collective-permute-start.16 = (bf16[8,16,512]{2,1,0:T(8,128)(2,1)S(1)}, bf16[8,16,512]{2,1,0:T(8,128)(2,1)S(1)}, u32[]{:S(2)}, u32[]{:S(2)}) collective-permute-start(bf16[8,16,512]{2,1,0:T(8,128)(2,1)S(1)} %constant_dynamic-update-slice_fusion.16), channel_id=1, source_target_pairs={{0,8},{8,16},{16,24},{24,32},{32,40},{40,48},{48,56},{56,64},{64,7... | collective-permute-start | bytes 393224 | tf_op jit(solution)/shard_map/ppermute | solution.py:284
  68.5 19.5 %collective-permute-done.16.refs_8_ = bf16[8,16,512]{2,1,0:T(8,128)(2,1)S(1)} collective-permute-done((bf16[8,16,512]{2,1,0:T(8,128)(2,1)S(1)}, bf16[8,16,512]{2,1,0:T(8,128)(2,1)S(1)}, u32[]{:S(2)}, u32[]{:S(2)}) %collective-permute-start.16) | collective-permute-done | bytes 131104 | tf_op jit(solution)/shard_map/ppermute | solution.py:284
  88.5 2.1 collective-permute-start.18
  90.6 11.2 %collective-permute-done.17.refs_11_ = bf16[4,128,512]{2,1,0:T(8,128)(2,1)S(1)} collective-permute-done((bf16[4,128,512]{2,1,0:T(8,128)(2,1)S(1)}, bf16[4,128,512]{2,1,0:T(8,128)(2,1)S(1)}, u32[]{:S(2)}, u32[]{:S(2)}) %collective-permute-start.17) | collective-permute-done | bytes 524320 | tf_op jit(solution)/shard_map/ppermute | solution.py:235
  102.6 3.0 %collective-permute-start.19 = (bf16[8,128,512]{2,1,0:T(8,128)(2,1)S(1)}, bf16[8,128,512]{2,1,0:T(8,128)(2,1)}, u32[]{:S(2)}, u32[]{:S(2)}) collective-permute-start(bf16[8,128,512]{2,1,0:T(8,128)(2,1)S(1)} %get-tuple-element.61.refs_8_), channel_id=1, source_target_pairs={{8,0},{16,8},{24,16},{0,24},{9,1},{17,9},{25,17},{1,25},{10,2},{18... | collective-permute-start | bytes 3145736 | tf_op jit(solution)/shard_map/ppermute | solution.py:235
  105.6 1.6 copy.13.refs_17_.step
  107.9 17.1 %raw.1 = (bf16[768,768]{1,0:T(8,128)(2,1)}, bf16[32,8,512]{2,1,0:T(8,128)(2,1)}) custom-call(s32[4]{0:T(128)} %pad_add_fusion.place, bf16[768,512]{1,0:T(8,128)(2,1)} %refs_0_.1, bf16[768,512]{1,0:T(8,128)(2,1)} %copy-done.4, bf16[768,512]{1,0:T(8,128)(2,1)} %collective-permute-done.2.refs_2_, bf16[768,512]{1,0:T(8,128)(2,1)} %copy-done.6, ...), custom_call_target="tpu_custom_call" | custom-call | tf_op jit(solution)/shard_map/raw/pallas_call | solution.py:295
  125.0 12.0 %all-to-all-start = ((bf16[32,8,512]{2,1,0:T(8,128)(2,1)}), bf16[32,8,512]{2,1,0:T(8,128)(2,1)S(1)}, u32[]{:S(2)}, u32[]{:S(2)}) async-start(bf16[32,8,512]{2,1,0:T(8,128)(2,1)} %get-tuple-element.60), calls=%async_computation | async-start | bytes 524288 | tf_op jit(solution)/shard_map/all_to_all | solution.py:320
  139.5 12.3 %collective-permute-start.22 = (bf16[4,128,512]{2,1,0:T(8,128)(2,1)S(1)}, bf16[4,128,512]{2,1,0:T(8,128)(2,1)S(1)}, u32[]{:S(2)}, u32[]{:S(2)}) collective-permute-start(bf16[4,128,512]{2,1,0:T(8,128)(2,1)S(1)} %slice.55), channel_id=1, source_target_pairs={{24,0},{0,8},{8,16},{16,24},{25,1},{1,9},{9,17},{17,25},{26,2},{2,... | collective-permute-start | bytes 1572872 | tf_op jit(solution)/shard_map/ppermute | solution.py:235
  151.8 8.4 %scan.1.earlier.output = f32[768,512]{1,0:T(8,128)} custom-call(bf16[768,768]{1,0:T(8,128)(2,1)} %get-tuple-element.59.conv, f32[768,8]{1,0:T(8,128)} %copy.13.refs_17_.step, f32[1,8]{1,0:T(1,128)} %bitcast.44, f32[1,8]{1,0:T(1,128)} %bitcast.47), custom_call_target="tpu_custom_call" | custom-call | tf_op jit(solution)/shard_map/scan/pallas_call | solution.py:323
  160.9 1.8 prefix.1
  162.7 10.7 %all-to-all-start.1 = ((bf16[32,4,512]{2,1,0:T(4,128)(2,1)}), bf16[32,4,512]{2,1,0:T(4,128)(2,1)S(1)}, u32[]{:S(2)}, u32[]{:S(2)}) async-start(bf16[32,4,512]{2,1,0:T(4,128)(2,1)} %prefix.1), calls=%async_computation.1 | async-start | bytes 262144 | tf_op jit(solution)/shard_map/all_to_all | solution.py:338
  174.9 8.9 %gate.1 = bf16[768,512]{1,0:T(8,128)(2,1)} custom-call(s32[4]{0:T(128)} %pad_add_fusion.place, bf16[768,512]{1,0:T(8,128)(2,1)} %refs_0_.1, bf16[768,512]{1,0:T(8,128)(2,1)} %copy-done.4, bf16[768,512]{1,0:T(8,128)(2,1)} %collective-permute-done.2.refs_2_, bf16[768,512]{1,0:T(8,128)(2,1)} %copy-done.6, bf16[768,512]{1,0:T(8,128)(2,1)} %copy-done.8, ...), custom_call_target="tpu_custom_call" | custom-call | tf_op jit(solution)/shard_map/gate/pallas_call | solution.py:340
  184.5 6.3 %norm.1.own.earlier = bf16[768,512]{1,0:T(8,128)(2,1)} custom-call(f32[768,512]{1,0:T(8,128)} %scan.1.earlier.output, bf16[768,768]{1,0:T(8,128)(2,1)} %get-tuple-element.59.conv, f32[768,8]{1,0:T(8,128)} %copy.13.refs_17_.step, f32[1,8]{1,0:T(1,128)} %bitcast.45, bf16[32,4,512]{2,1,0:T(4,128)(2,1)} %copy-done.22, bf16[768,512]{1,0:T(8,128)(2,1)} %gate.1, ...), custom_call_target="tpu_custom_call" | custom-call | tf_op jit(solution)/shard_map/norm/pallas_call | solution.py:356
  191.4 1.9 collective-permute-done.23.sibling
  194.2 4.4 %out.3 = (bf16[384,512]{1,0:T(8,128)(2,1)}, bf16[384,512]{1,0:T(8,128)(2,1)}) custom-call(s32[6]{0:T(128)} %stack.107.targets, bf16[768,512]{1,0:T(8,128)(2,1)} %norm.1.own.earlier, bf16[768,512]{1,0:T(8,128)(2,1)} %copy-done, bf16[4096,512]{1,0:T(8,128)(2,1)} %all-gather.7.cloned.1.call-done.w_own.w_sibling, ...), custom_call_target="tpu_custom_call" | custom-call | flops 805306368 | bytes 1048576 | tf_op jit(solution)/shard_map/out/pallas_call | solution.py:373
  199.2 3.2 %collective-permute-start.24 = (bf16[384,512]{1,0:T(8,128)(2,1)}, bf16[384,512]{1,0:T(8,128)(2,1)S(1)}, u32[]{:S(2)}, u32[]{:S(2)}) collective-permute-start(bf16[384,512]{1,0:T(8,128)(2,1)} %get-tuple-element.65.earlier), channel_id=1, source_target_pairs={{6,0},{0,2},{2,4},{4,6},{7,1},{1,3},{3,5},{5,7},{14,8},{8,10},{10,... | collective-permute-start | bytes 1179656 | tf_op jit(solution)/shard_map/ppermute | solution.py:235
  202.5 7.2 %out.4 = (bf16[384,512]{1,0:T(8,128)(2,1)}, bf16[384,512]{1,0:T(8,128)(2,1)}, f32[384,512]{1,0:T(8,128)}, f32[384,512]{1,0:T(8,128)}) custom-call(s32[12]{0:T(128)} %stack.104.targets, bf16[768,512]{1,0:T(8,128)(2,1)} %norm.1.own.earlier, bf16[768,512]{1,0:T(8,128)(2,1)} %copy-done, bf16[4096,512]{1,0:T(8,128)(2,1)} %all-gather.7.cloned.1.call-done.w_own.w_sibling, ...), custom_call_target="tpu_custom_call" | custom-call | flops 1610612736 | bytes 2097152 | tf_op jit(solution)/shard_map/out/pallas_call | solution.py:373
  209.7 1.4 collective-permute-done.28
  213.3 3.2 %collective-permute-start.26 = (bf16[384,512]{1,0:T(8,128)(2,1)S(1)}, bf16[384,512]{1,0:T(8,128)(2,1)S(1)}, u32[]{:S(2)}, u32[]{:S(2)}) collective-permute-start(bf16[384,512]{1,0:T(8,128)(2,1)S(1)} %add_convert_fusion.3.earlier), channel_id=1, source_target_pairs={{6,0},{0,2},{2,4},{4,6},{7,1},{1,3},{3,5},{5,7},{14,8},{8,10},{10,... | collective-permute-start | bytes 1179656 | tf_op jit(solution)/shard_map/ppermute | solution.py:235
  217.2 4.7 %out.5 = (f32[384,512]{1,0:T(8,128)}, f32[384,512]{1,0:T(8,128)}) custom-call(s32[6]{0:T(128)} %stack.85.targets, bf16[768,512]{1,0:T(8,128)(2,1)} %norm.1.own.earlier, bf16[768,512]{1,0:T(8,128)(2,1)} %copy-done, bf16[4096,512]{1,0:T(8,128)(2,1)} %all-gather.7.cloned.1.call-done.w_own.w_sibling, ...), custom_call_target="tpu_custom_call" | custom-call | flops 805306368 | bytes 1048576 | tf_op jit(solution)/shard_map/out/pallas_call | solution.py:373
  222.0 3.7 %collective-permute-done.29 = bf16[384,512]{1,0:T(8,128)(2,1)S(1)} collective-permute-done((bf16[384,512]{1,0:T(8,128)(2,1)S(1)}, bf16[384,512]{1,0:T(8,128)(2,1)S(1)}, u32[]{:S(2)}, u32[]{:S(2)}) %collective-permute-start.29) | collective-permute-done | bytes 393248 | tf_op jit(solution)/shard_map/ppermute | solution.py:235
  227.0 5.4 %collective-permute-done.25 = bf16[384,512]{1,0:T(8,128)(2,1)S(1)} collective-permute-done((bf16[384,512]{1,0:T(8,128)(2,1)S(1)}, bf16[384,512]{1,0:T(8,128)(2,1)S(1)}, u32[]{:S(2)}, u32[]{:S(2)}) %collective-permute-start.25) | collective-permute-done | bytes 393248 | tf_op jit(solution)/shard_map/ppermute | solution.py:235
  (145 shorter events, 29.4 us)
Async XLA Ops:
  6.5 49.2 %all-gather.9.cloned.1.call-start = ((), (), s32[]{:S(2)}) async-start(), calls=%async_computation.4 | async-start | bytes 2359296 | tf_op jit(solution)/shard_map/all_gather | solution.py:267
  8.3 99.5 %all-gather.5.cloned.1.call-start = ((), (), s32[]{:S(2)}) async-start(), calls=%async_computation.2 | async-start | bytes 2359296 | tf_op jit(solution)/shard_map/all_gather | solution.py:277
  8.4 5.9 %collective-permute-start.3 = (bf16[128,256]{1,0:T(8,128)(2,1)}, bf16[128,256]{1,0:T(8,128)(2,1)S(1)}, u32[]{:S(2)}, u32[]{:S(2)}) collective-permute-start(bf16[128,256]{1,0:T(8,128)(2,1)} %param.14), channel_id=1, source_target_pairs={{8,0},{16,8},{24,16},{0,24},{9,1},{17,9},{25,17},{1,25},{10,2},{18... | collective-permute-start | bytes 196616 | tf_op jit(solution)/shard_map/ppermute | solution.py:235
  8.9 6.0 %collective-permute-start.4 = (bf16[128,256]{1,0:T(8,128)(2,1)}, bf16[128,256]{1,0:T(8,128)(2,1)S(1)}, u32[]{:S(2)}, u32[]{:S(2)}) collective-permute-start(bf16[128,256]{1,0:T(8,128)(2,1)} %param.14), channel_id=1, source_target_pairs={{16,0},{24,8},{0,16},{8,24},{17,1},{25,9},{1,17},{9,25},{18,2},{26... | collective-permute-start | bytes 196616 | tf_op jit(solution)/shard_map/ppermute | solution.py:235
  11.5 4.5 %collective-permute-start.5 = (bf16[128,256]{1,0:T(8,128)(2,1)}, bf16[128,256]{1,0:T(8,128)(2,1)S(1)}, u32[]{:S(2)}, u32[]{:S(2)}) collective-permute-start(bf16[128,256]{1,0:T(8,128)(2,1)} %param.14), channel_id=1, source_target_pairs={{24,0},{0,8},{8,16},{16,24},{25,1},{1,9},{9,17},{17,25},{26,2},{2,... | collective-permute-start | bytes 196616 | tf_op jit(solution)/shard_map/ppermute | solution.py:235
  17.6 175.7 %all-gather.7.cloned.1.call-start = ((), (), s32[]{:S(2)}) async-start(), calls=%async_computation.3 | async-start | bytes 4718592 | tf_op jit(solution)/shard_map/all_gather | solution.py:285
  17.7 19.4 %collective-permute-start = (bf16[768,512]{1,0:T(8,128)(2,1)S(1)}, bf16[768,512]{1,0:T(8,128)(2,1)S(1)}, u32[]{:S(2)}, u32[]{:S(2)}) collective-permute-start(bf16[768,512]{1,0:T(8,128)(2,1)S(1)} %copy-done.3), channel_id=1, source_target_pairs={{2,0},{4,2},{6,4},{0,6},{3,1},{5,3},{7,5},{1,7},{10,8},{12,10},{14... | collective-permute-start | bytes 2359304 | tf_op jit(solution)/shard_map/ppermute | solution.py:235
  19.4 7.2 %collective-permute-start.7 = (bf16[128,512]{1,0:T(8,128)(2,1)S(1)}, bf16[128,512]{1,0:T(8,128)(2,1)S(1)}, u32[]{:S(2)}, u32[]{:S(2)}) collective-permute-start(bf16[128,512]{1,0:T(8,128)(2,1)S(1)} %collective-permute-done.6), channel_id=1, source_target_pairs={{8,0},{16,8},{24,16},{0,24},{9,1},{17,9},{25,17},{1,25},{10,2},{18... | collective-permute-start | bytes 393224 | tf_op jit(solution)/shard_map/ppermute | solution.py:235
  22.1 16.1 %collective-permute-start.1 = (bf16[768,512]{1,0:T(8,128)(2,1)S(1)}, bf16[768,512]{1,0:T(8,128)(2,1)S(1)}, u32[]{:S(2)}, u32[]{:S(2)}) collective-permute-start(bf16[768,512]{1,0:T(8,128)(2,1)S(1)} %copy-done.3), channel_id=1, source_target_pairs={{6,0},{0,2},{2,4},{4,6},{7,1},{1,3},{3,5},{5,7},{14,8},{8,10},{10,... | collective-permute-start | bytes 2359304 | tf_op jit(solution)/shard_map/ppermute | solution.py:235
  24.5 12.6 %collective-permute-start.8 = (bf16[128,512]{1,0:T(8,128)(2,1)S(1)}, bf16[128,512]{1,0:T(8,128)(2,1)S(1)}, u32[]{:S(2)}, u32[]{:S(2)}) collective-permute-start(bf16[128,512]{1,0:T(8,128)(2,1)S(1)} %collective-permute-done.6), channel_id=1, source_target_pairs={{16,0},{24,8},{0,16},{8,24},{17,1},{25,9},{1,17},{9,25},{18,2},{26... | collective-permute-start | bytes 393224 | tf_op jit(solution)/shard_map/ppermute | solution.py:235
  25.2 11.9 %collective-permute-start.9 = (bf16[128,512]{1,0:T(8,128)(2,1)S(1)}, bf16[128,512]{1,0:T(8,128)(2,1)S(1)}, u32[]{:S(2)}, u32[]{:S(2)}) collective-permute-start(bf16[128,512]{1,0:T(8,128)(2,1)S(1)} %collective-permute-done.6), channel_id=1, source_target_pairs={{24,0},{0,8},{8,16},{16,24},{25,1},{1,9},{9,17},{17,25},{26,2},{2,... | collective-permute-start | bytes 393224 | tf_op jit(solution)/shard_map/ppermute | solution.py:235
  37.1 18.6 %collective-permute-start.2 = (bf16[768,512]{1,0:T(8,128)(2,1)S(1)}, bf16[768,512]{1,0:T(8,128)(2,1)}, u32[]{:S(2)}, u32[]{:S(2)}) collective-permute-start(bf16[768,512]{1,0:T(8,128)(2,1)S(1)} %collective-permute-done.refs_1_), channel_id=1, source_target_pairs={{2,0},{4,2},{6,4},{0,6},{3,1},{5,3},{7,5},{1,7},{10,8},{12,10},{14... | collective-permute-start | bytes 2359304 | tf_op jit(solution)/shard_map/ppermute | solution.py:235
  55.7 5.6 %collective-permute-start.12 = (bf16[768,512]{1,0:T(8,128)(2,1)S(1)}, bf16[768,512]{1,0:T(8,128)(2,1)S(1)}, u32[]{:S(2)}, u32[]{:S(2)}) collective-permute-start(bf16[768,512]{1,0:T(8,128)(2,1)S(1)} %copy-done.3), channel_id=1, source_target_pairs={{1,0},{0,1},{3,2},{2,3},{5,4},{4,5},{7,6},{6,7},{9,8},{8,9},{11,10... | collective-permute-start | bytes 2359304 | tf_op jit(solution)/shard_map/ppermute | solution.py:235
  57.8 30.3 %collective-permute-start.10 = (bf16[8,128,512]{2,1,0:T(8,128)(2,1)S(1)}, bf16[8,128,512]{2,1,0:T(8,128)(2,1)S(1)}, u32[]{:S(2)}, u32[]{:S(2)}) collective-permute-start(bf16[8,128,512]{2,1,0:T(8,128)(2,1)S(1)} %get-tuple-element.74.refs_9_), channel_id=1, source_target_pairs={{8,0},{16,8},{24,16},{0,24},{9,1},{17,9},{25,17},{1,25},{10,2},{18... | collective-permute-start | bytes 3145736 | tf_op jit(solution)/shard_map/ppermute | solution.py:235
  59.9 28.1 %collective-permute-start.11 = (bf16[8,128,512]{2,1,0:T(8,128)(2,1)S(1)}, bf16[8,128,512]{2,1,0:T(8,128)(2,1)S(1)}, u32[]{:S(2)}, u32[]{:S(2)}) collective-permute-start(bf16[8,128,512]{2,1,0:T(8,128)(2,1)S(1)} %get-tuple-element.74.refs_9_), channel_id=1, source_target_pairs={{24,0},{0,8},{8,16},{16,24},{25,1},{1,9},{9,17},{17,25},{26,2},{2,... | collective-permute-start | bytes 3145736 | tf_op jit(solution)/shard_map/ppermute | solution.py:235
  60.3 3.4 %collective-permute-start.14 = (bf16[768,512]{1,0:T(8,128)(2,1)}, bf16[768,512]{1,0:T(8,128)(2,1)S(1)}, u32[]{:S(2)}, u32[]{:S(2)}) collective-permute-start(bf16[768,512]{1,0:T(8,128)(2,1)} %collective-permute-done.2.refs_2_), channel_id=1, source_target_pairs={{1,0},{0,1},{3,2},{2,3},{5,4},{4,5},{7,6},{6,7},{9,8},{8,9},{11,10... | collective-permute-start | bytes 2359304 | tf_op jit(solution)/shard_map/ppermute | solution.py:235
  61.4 3.3 %collective-permute-start.15 = (bf16[768,512]{1,0:T(8,128)(2,1)S(1)}, bf16[768,512]{1,0:T(8,128)(2,1)S(1)}, u32[]{:S(2)}, u32[]{:S(2)}) collective-permute-start(bf16[768,512]{1,0:T(8,128)(2,1)S(1)} %copy-done.7), channel_id=1, source_target_pairs={{1,0},{0,1},{3,2},{2,3},{5,4},{4,5},{7,6},{6,7},{9,8},{8,9},{11,10... | collective-permute-start | bytes 2359304 | tf_op jit(solution)/shard_map/ppermute | solution.py:235
  64.7 23.3 %collective-permute-start.16 = (bf16[8,16,512]{2,1,0:T(8,128)(2,1)S(1)}, bf16[8,16,512]{2,1,0:T(8,128)(2,1)S(1)}, u32[]{:S(2)}, u32[]{:S(2)}) collective-permute-start(bf16[8,16,512]{2,1,0:T(8,128)(2,1)S(1)} %constant_dynamic-update-slice_fusion.16), channel_id=1, source_target_pairs={{0,8},{8,16},{16,24},{24,32},{32,40},{40,48},{48,56},{56,64},{64,7... | collective-permute-start | bytes 393224 | tf_op jit(solution)/shard_map/ppermute | solution.py:284
  88.1 13.6 %collective-permute-start.17 = (bf16[4,128,512]{2,1,0:T(8,128)(2,1)S(1)}, bf16[4,128,512]{2,1,0:T(8,128)(2,1)S(1)}, u32[]{:S(2)}, u32[]{:S(2)}) collective-permute-start(bf16[4,128,512]{2,1,0:T(8,128)(2,1)S(1)} %slice.51), channel_id=1, source_target_pairs={{8,0},{16,8},{24,16},{0,24},{9,1},{17,9},{25,17},{1,25},{10,2},{18... | collective-permute-start | bytes 1572872 | tf_op jit(solution)/shard_map/ppermute | solution.py:235
  88.5 14.1 %collective-permute-start.18 = (bf16[4,128,512]{2,1,0:T(8,128)(2,1)S(1)}, bf16[4,128,512]{2,1,0:T(8,128)(2,1)S(1)}, u32[]{:S(2)}, u32[]{:S(2)}) collective-permute-start(bf16[4,128,512]{2,1,0:T(8,128)(2,1)S(1)} %slice.52), channel_id=1, source_target_pairs={{24,0},{0,8},{8,16},{16,24},{25,1},{1,9},{9,17},{17,25},{26,2},{2,... | collective-permute-start | bytes 1572872 | tf_op jit(solution)/shard_map/ppermute | solution.py:235
  102.6 34.5 %collective-permute-start.19 = (bf16[8,128,512]{2,1,0:T(8,128)(2,1)S(1)}, bf16[8,128,512]{2,1,0:T(8,128)(2,1)}, u32[]{:S(2)}, u32[]{:S(2)}) collective-permute-start(bf16[8,128,512]{2,1,0:T(8,128)(2,1)S(1)} %get-tuple-element.61.refs_8_), channel_id=1, source_target_pairs={{8,0},{16,8},{24,16},{0,24},{9,1},{17,9},{25,17},{1,25},{10,2},{18... | collective-permute-start | bytes 3145736 | tf_op jit(solution)/shard_map/ppermute | solution.py:235
  105.5 31.5 %collective-permute-start.20 = (bf16[8,128,512]{2,1,0:T(8,128)(2,1)S(1)}, bf16[8,128,512]{2,1,0:T(8,128)(2,1)}, u32[]{:S(2)}, u32[]{:S(2)}) collective-permute-start(bf16[8,128,512]{2,1,0:T(8,128)(2,1)S(1)} %get-tuple-element.61.refs_8_), channel_id=1, source_target_pairs={{24,0},{0,8},{8,16},{16,24},{25,1},{1,9},{9,17},{17,25},{26,2},{2,... | collective-permute-start | bytes 3145736 | tf_op jit(solution)/shard_map/ppermute | solution.py:235
  125.0 35.2 %all-to-all-start = ((bf16[32,8,512]{2,1,0:T(8,128)(2,1)}), bf16[32,8,512]{2,1,0:T(8,128)(2,1)S(1)}, u32[]{:S(2)}, u32[]{:S(2)}) async-start(bf16[32,8,512]{2,1,0:T(8,128)(2,1)} %get-tuple-element.60), calls=%async_computation | async-start | bytes 524288 | tf_op jit(solution)/shard_map/all_to_all | solution.py:320
  138.1 35.2 %collective-permute-start.21 = (bf16[4,128,512]{2,1,0:T(8,128)(2,1)S(1)}, bf16[4,128,512]{2,1,0:T(8,128)(2,1)S(1)}, u32[]{:S(2)}, u32[]{:S(2)}) collective-permute-start(bf16[4,128,512]{2,1,0:T(8,128)(2,1)S(1)} %slice.54), channel_id=1, source_target_pairs={{8,0},{16,8},{24,16},{0,24},{9,1},{17,9},{25,17},{1,25},{10,2},{18... | collective-permute-start | bytes 1572872 | tf_op jit(solution)/shard_map/ppermute | solution.py:235
  139.5 33.8 %collective-permute-start.22 = (bf16[4,128,512]{2,1,0:T(8,128)(2,1)S(1)}, bf16[4,128,512]{2,1,0:T(8,128)(2,1)S(1)}, u32[]{:S(2)}, u32[]{:S(2)}) collective-permute-start(bf16[4,128,512]{2,1,0:T(8,128)(2,1)S(1)} %slice.55), channel_id=1, source_target_pairs={{24,0},{0,8},{8,16},{16,24},{25,1},{1,9},{9,17},{17,25},{26,2},{2,... | collective-permute-start | bytes 1572872 | tf_op jit(solution)/shard_map/ppermute | solution.py:235
  162.7 21.2 %all-to-all-start.1 = ((bf16[32,4,512]{2,1,0:T(4,128)(2,1)}), bf16[32,4,512]{2,1,0:T(4,128)(2,1)S(1)}, u32[]{:S(2)}, u32[]{:S(2)}) async-start(bf16[32,4,512]{2,1,0:T(4,128)(2,1)} %prefix.1), calls=%async_computation.1 | async-start | bytes 262144 | tf_op jit(solution)/shard_map/all_to_all | solution.py:338
  198.5 12.6 %collective-permute-start.28 = (bf16[384,512]{1,0:T(8,128)(2,1)}, bf16[384,512]{1,0:T(8,128)(2,1)S(1)}, u32[]{:S(2)}, u32[]{:S(2)}) collective-permute-start(bf16[384,512]{1,0:T(8,128)(2,1)} %get-tuple-element.72), channel_id=1, source_target_pairs={{2,0},{4,2},{6,4},{0,6},{3,1},{5,3},{7,5},{1,7},{10,8},{12,10},{14... | collective-permute-start | bytes 1179656 | tf_op jit(solution)/shard_map/ppermute | solution.py:235
  199.2 14.0 %collective-permute-start.24 = (bf16[384,512]{1,0:T(8,128)(2,1)}, bf16[384,512]{1,0:T(8,128)(2,1)S(1)}, u32[]{:S(2)}, u32[]{:S(2)}) collective-permute-start(bf16[384,512]{1,0:T(8,128)(2,1)} %get-tuple-element.65.earlier), channel_id=1, source_target_pairs={{6,0},{0,2},{2,4},{4,6},{7,1},{1,3},{3,5},{5,7},{14,8},{8,10},{10,... | collective-permute-start | bytes 1179656 | tf_op jit(solution)/shard_map/ppermute | solution.py:235
  209.6 12.3 %collective-permute-start.27 = (bf16[384,512]{1,0:T(8,128)(2,1)}, bf16[384,512]{1,0:T(8,128)(2,1)S(1)}, u32[]{:S(2)}, u32[]{:S(2)}) collective-permute-start(bf16[384,512]{1,0:T(8,128)(2,1)} %get-tuple-element.70), channel_id=1, source_target_pairs={{6,0},{0,2},{2,4},{4,6},{7,1},{1,3},{3,5},{5,7},{14,8},{8,10},{10,... | collective-permute-start | bytes 1179656 | tf_op jit(solution)/shard_map/ppermute | solution.py:235
  212.4 13.3 %collective-permute-start.29 = (bf16[384,512]{1,0:T(8,128)(2,1)S(1)}, bf16[384,512]{1,0:T(8,128)(2,1)S(1)}, u32[]{:S(2)}, u32[]{:S(2)}) collective-permute-start(bf16[384,512]{1,0:T(8,128)(2,1)S(1)} %add_convert_fusion.1), channel_id=1, source_target_pairs={{2,0},{4,2},{6,4},{0,6},{3,1},{5,3},{7,5},{1,7},{10,8},{12,10},{14... | collective-permute-start | bytes 1179656 | tf_op jit(solution)/shard_map/ppermute | solution.py:235
  213.1 19.3 %collective-permute-start.25 = (bf16[384,512]{1,0:T(8,128)(2,1)S(1)}, bf16[384,512]{1,0:T(8,128)(2,1)S(1)}, u32[]{:S(2)}, u32[]{:S(2)}) collective-permute-start(bf16[384,512]{1,0:T(8,128)(2,1)S(1)} %copy-done.25), channel_id=1, source_target_pairs={{2,0},{4,2},{6,4},{0,6},{3,1},{5,3},{7,5},{1,7},{10,8},{12,10},{14... | collective-permute-start | bytes 1179656 | tf_op jit(solution)/shard_map/ppermute | solution.py:235
  213.3 19.1 %collective-permute-start.26 = (bf16[384,512]{1,0:T(8,128)(2,1)S(1)}, bf16[384,512]{1,0:T(8,128)(2,1)S(1)}, u32[]{:S(2)}, u32[]{:S(2)}) collective-permute-start(bf16[384,512]{1,0:T(8,128)(2,1)S(1)} %add_convert_fusion.3.earlier), channel_id=1, source_target_pairs={{6,0},{0,2},{2,4},{4,6},{7,1},{1,3},{3,5},{5,7},{14,8},{8,10},{10,... | collective-permute-start | bytes 1179656 | tf_op jit(solution)/shard_map/ppermute | solution.py:235
  (29 other events, 415.5 us)
Sparse Core Ops, SparseCore 0:
  9.1 44.5 all-gather.8
  55.5 39.8 all-gather.4
  97.2 60.8 all-gather.6

commit v3 on v2

v3 whole, which is shorter than its diff:
```python
import jax
import jax.numpy as jnp
from jax import lax
from jax.experimental import pallas as pl
from jax.experimental.pallas import tpu as pltpu
from jax.sharding import Mesh, PartitionSpec as P

F32 = jnp.float32
BF16 = jnp.bfloat16

P_SIZE = 64
N = 128
TAPS = 4
HALO = 16
BLOCK = 128
CONTEXT = ("z", "y")
TENSOR = ("x", "core")


def params(mebibytes):
    return pltpu.CompilerParams(vmem_limit_bytes=mebibytes * 1024 * 1024)


def cost(flops, bytes_accessed):
    return pl.CostEstimate(flops=flops, bytes_accessed=bytes_accessed, transcendentals=0)


def parts(v, count):
    found = []
    for _ in range(count):
        found.append(v.astype(BF16).astype(F32))
        v = v - found[-1]
    return jnp.concatenate(found, axis=0).astype(BF16)


def by_column(v, width):
    heads = v.shape[0]
    head = lax.broadcasted_iota(jnp.int32, (2 * heads, width), 0) % heads
    column = lax.broadcasted_iota(jnp.int32, (2 * heads, width), 1)
    spread = (column // P_SIZE == head).astype(F32).astype(BF16)
    return dot(parts(v, 2), spread, ((0,), (0,)))


def running_sum(v):
    heads, rows = v.shape
    r = lax.broadcasted_iota(jnp.int32, (rows, rows), 0)
    c = lax.broadcasted_iota(jnp.int32, (rows, rows), 1)
    sums = dot(parts(v, 3), (r <= c).astype(F32).astype(BF16))
    return sums[:heads] + sums[heads : 2 * heads] + sums[2 * heads :]


def dot(a, b, contract=((1,), (0,))):
    return lax.dot_general(a, b, (contract, ((), ())), preferred_element_type=F32)


def silu(v):
    return 0.5 * v * (1.0 + jnp.tanh(0.5 * v))


def decays(step, rate, width):
    run = running_sum(-step * rate)
    last = run[:, run.shape[1] - 1 :]
    mid = 0.5 * last
    grow = by_column(jnp.exp(run - mid), width)
    shrink = by_column(step * jnp.exp(mid - run), width)
    ends = jnp.concatenate([jnp.exp(mid), jnp.exp(last - mid), jnp.exp(last), last] * 2, axis=1)
    return grow, shrink, by_column(ends, width)


def block_of(place, piece):
    x, core = place[2], place[3]
    other = piece // 4
    return lax.rem(x + piece % 4, 4) * 2 + (core if other == 0 else 1 - core)


def quarter_at(y, distance, rows):
    return pl.ds(pl.multiple_of(lax.rem(y + distance, 4) * rows, rows), rows)


def split_copy(block, first, rest, target, sem):
    half = first.shape[0]

    @pl.when(block < half)
    def _():
        pltpu.make_async_copy(first.at[block], target, sem).start()

    @pl.when(block >= half)
    def _():
        pltpu.make_async_copy(rest.at[block - half], target, sem).start()


def staged(start, finish):
    for i in range(3):
        start(i)
    for i in range(8):
        finish(i)
        if i + 3 < 8:
            start(i + 3)


def raw_kernel(place, *refs):
    pieces, refs = refs[:8], refs[8:]
    v0, rest0, v1, rest1, v3, rest3, out, tok, wv, tok_sems, v_sems = refs
    y = place[1]
    quarter = v0.shape[1]

    def start(i):
        pltpu.make_async_copy(pieces[i], tok.at[i], tok_sems.at[i]).start()
        for d, first, rest in ((0, v0, rest0), (1, v1, rest1), (3, v3, rest3)):
            target = wv.at[i, quarter_at(y, d, quarter)]
            split_copy(block_of(place, i), first, rest, target, v_sems.at[i, d])
        wv[i, quarter_at(y, 2, quarter), :] = jnp.zeros((quarter, wv.shape[2]), BF16)

    def finish(i):
        pltpu.make_async_copy(pieces[i], tok.at[i], tok_sems.at[i]).wait()
        for d in (0, 1, 3):
            target = wv.at[i, quarter_at(y, d, quarter)]
            pltpu.make_async_copy(v0.at[0], target, v_sems.at[i, d]).wait()
        part = dot(tok[i], wv[i])
        out[...] = part if i == 0 else out[...] + part

    staged(start, finish)


def conv_kernel(place, *refs):
    pieces, refs = refs[:8], refs[8:]
    across, across_rest, keys, value_part, taps_v, taps_k, step, rate, *refs = refs
    conv_out, packed_out, tok, wk, wv, acc, tok_sems, k_sems, v_sems = refs
    depth = tok.shape[2]
    value = taps_v.shape[1]
    y = place[1]
    quarter = across.shape[1]

    def copies(i):
        yield pltpu.make_async_copy(pieces[i], tok.at[i], tok_sems.at[i])
        at = pl.ds(pl.multiple_of(block_of(place, i) * depth, depth), depth)
        yield pltpu.make_async_copy(keys.at[at], wk.at[i], k_sems.at[i])

    def start(i):
        for copy in copies(i):
            copy.start()
        target = wv.at[pl.ds(i * quarter, quarter)]
        split_copy(block_of(place, i), across, across_rest, target, v_sems.at[i])

    def finish(i):
        for copy in copies(i):
            copy.wait()
        target = wv.at[pl.ds(i * quarter, quarter)]
        pltpu.make_async_copy(across.at[0], target, v_sems.at[i]).wait()
        key_part = dot(tok[i], wk[i])
        acc[:, value:] = key_part if i == 0 else acc[:, value:] + key_part

    staged(start, finish)
    mine = [tok[i, :, quarter_at(y, 2, quarter)] for i in range(8)]
    acc[:, :value] = value_part[...] + dot(jnp.concatenate(mine, axis=1), wv[...])
    acc[...] = acc[...].astype(BF16).astype(F32)
    taps = jnp.concatenate([taps_v[...], taps_k[...]], axis=1)
    state = jnp.zeros((N, value), F32)
    total = jnp.zeros((1, value), F32)
    for b in range(step.shape[1] // BLOCK):
        first = b * BLOCK
        summed = jnp.zeros((BLOCK, acc.shape[1]), F32)
        for tap in range(TAPS):
            start = HALO - (TAPS - 1) + first + tap
            summed = summed + taps[tap : tap + 1] * acc[start : start + BLOCK, :]
        convolved = silu(summed).astype(BF16)
        conv_out[first : first + BLOCK, :] = convolved
        _, shrink, ends = decays(step[:, first : first + BLOCK], rate[...], value)
        signal = (convolved[:, :value].astype(F32) * shrink).astype(BF16)
        fresh = dot(convolved[:, value : value + N], signal, ((0,), (0,)))
        state = ends[2:3] * state + ends[1:2] * fresh
        total = total + ends[3:4]
    high = total.astype(BF16).astype(F32)
    middle = (total - high).astype(BF16).astype(F32)
    low = total - high - middle
    totals = jnp.concatenate([high, middle, low, jnp.zeros_like(low)], axis=0)
    for p in range(packed_out.shape[0]):
        slab = N // packed_out.shape[0]
        packed_out[p] = jnp.concatenate([state[p * slab : (p + 1) * slab], totals], axis=0).astype(BF16)


def prefix_kernel(states, earlier, out):
    pieces = states.shape[0]
    rows = out.shape[1]
    state = jnp.zeros((rows, out.shape[2]), F32)
    for piece in range(pieces):
        out[piece] = state.astype(BF16)
        block = states[piece].astype(F32)
        total = block[rows : rows + 1] + block[rows + 1 : rows + 2] + block[rows + 2 : rows + 3]
        state = jnp.exp(total) * state + block[:rows]


def scan_kernel(conv, step, rate, skip, out):
    value = out.shape[1]
    direct = by_column(jnp.broadcast_to(skip[...], step.shape[:1] + (8,)), value)[0:1]
    r = lax.broadcasted_iota(jnp.int32, (BLOCK, BLOCK), 0)
    c = lax.broadcasted_iota(jnp.int32, (BLOCK, BLOCK), 1)
    state = jnp.zeros((N, value), F32)
    for b in range(step.shape[1] // BLOCK):
        rows = slice(b * BLOCK, (b + 1) * BLOCK)
        grow, shrink, ends = decays(step[:, rows], rate[...], value)
        signal = conv[rows, :value].astype(F32)
        write = conv[rows, value : value + N]
        read = conv[rows, value + N :]
        scores = jnp.where(r >= c, dot(read, write, ((1,), (1,))), 0.0).astype(BF16)
        scaled = (signal * shrink).astype(BF16)
        left = jnp.concatenate([scores, read], axis=1)
        right = jnp.concatenate([scaled, (state * ends[0:1]).astype(BF16)], axis=0)
        out[rows, :] = grow * dot(left, right) + direct * signal
        state = ends[2:3] * state + ends[1:2] * dot(write, scaled, ((0,), (0,)))


def gate_kernel(place, *refs):
    pieces, refs = refs[:8], refs[8:]
    g0, g1, across, across_rest, g3, out, tok, wg, acc, tok_sems, w_sems = refs
    y = place[1]
    quarter = g0.shape[1]

    def copies(i):
        source = pieces[i].at[pl.ds(HALO, tok.shape[1])]
        yield pltpu.make_async_copy(source, tok.at[i], tok_sems.at[i])
        for d, source in ((0, g0), (1, g1), (3, g3)):
            target = wg.at[i, quarter_at(y, d, quarter)]
            yield pltpu.make_async_copy(source.at[block_of(place, i)], target, w_sems.at[i, d])

    def start(i):
        for copy in copies(i):
            copy.start()
        target = wg.at[i, quarter_at(y, 2, quarter)]
        split_copy(block_of(place, i), across, across_rest, target, w_sems.at[i, 2])

    def finish(i):
        for copy in copies(i):
            copy.wait()
        target = wg.at[i, quarter_at(y, 2, quarter)]
        pltpu.make_async_copy(across.at[0], target, w_sems.at[i, 2]).wait()
        part = dot(tok[i], wg[i])
        acc[...] = part if i == 0 else acc[...] + part

    staged(start, finish)
    out[...] = acc[...].astype(BF16)


def norm_kernel(output, conv, step, rate, start, gate, gain, normed):
    value = output.shape[1]
    so_far = jnp.zeros((step.shape[0], 1), F32)
    before = [start[p].astype(F32) for p in range(start.shape[0])]
    before = jnp.concatenate(before, axis=0).astype(BF16)
    for b in range(step.shape[1] // BLOCK):
        rows = slice(b * BLOCK, (b + 1) * BLOCK)
        run = so_far + running_sum(-step[:, rows] * rate[...])
        so_far = run[:, BLOCK - 1 :]
        kept = by_column(jnp.exp(run), value)
        total = output[rows, :] + kept * dot(conv[rows, value + N :], before)
        gated = total * silu(gate[rows, :].astype(F32))
        mean = jnp.mean(gated * gated, axis=1, keepdims=True)
        normed[rows, :] = (gated * lax.rsqrt(mean + 1e-05) * gain[...]).astype(BF16)


def out_kernel(targets, own, sibling, w_own, w_sibling, earlier, *outs):
    half = own.shape[0] // 2
    for part in range(2):
        rows = slice(part * half, (part + 1) * half)
        term = dot(own[rows, :], w_own[0]) + dot(sibling[rows, :], w_sibling[0])
        for job in range(len(outs) // 2):

            @pl.when(pl.program_id(0) == job)
            def _():
                out = outs[2 * job + part]
                out[...] = term.astype(out.dtype)


def shifted(array, axis, distance):
    size = lax.axis_size(axis)
    return lax.ppermute(array, axis, [((i + distance) % size, i) for i in range(size)])


def quad(array, dim=0):
    near = jnp.concatenate([array] + [shifted(array, "y", d) for d in (1, 2, 3)], axis=dim)
    return jnp.roll(near, lax.axis_index("y") * array.shape[dim], axis=dim)


def after(array, *others):
    return lax.optimization_barrier((array, *others))[0]


def local(
    tokens,
    w_gate,
    w_value,
    w_keys,
    conv_value,
    key_filter_taps,
    step,
    decay_rate,
    skip,
    norm_gain,
    w_out,
):
    rows, depth = tokens.shape
    value, keys = w_value.shape[1], w_keys.shape[1]
    step = step.T
    pieces = lax.axis_size(CONTEXT)
    shares = lax.axis_size(TENSOR)
    rate = decay_rate[:, None]

    both = lax.all_gather(jnp.concatenate([w_value, w_gate], axis=1), "z")
    keys_four = quad(w_keys)
    swap = []
    for z in range(8):
        for c in range(2):
            swap.append((2 * z + c, 2 * z + c if z % 2 == c else 2 * (z ^ 1) + 1 - c))
    swapped = lax.ppermute(after(w_out, keys_four), ("z", "core"), swap)
    outs_four = quad(swapped, 1)
    route = [(i, i + 1) for i in range(pieces - 1)]
    before = lax.ppermute(tokens[rows - HALO :], CONTEXT, route)
    own = jnp.concatenate([before, tokens], axis=0)
    ahead, behind = shifted(own, "x", 1), shifted(own, "x", -1)
    split = rows // 2 + HALO
    across = jnp.concatenate(
        [shifted(ahead[:split], "x", 1), shifted(behind[split:], "x", -1)], axis=0
    )
    keys_all = lax.all_gather(keys_four, "z", axis=0, tiled=True)
    other_near = [shifted(a, "core", 1) for a in (own, ahead, behind)]
    both, ahead, behind, across, outs_four, *other_near = after(
        (both, ahead, behind, across, outs_four, *other_near)
    )
    v0 = both[:4, :, :value], both[4:, :, :value]
    g0 = both[..., value:]
    v1_first, v3_rest = shifted(v0[0], "y", 1), shifted(v0[1], "y", -1)
    v1_rest, v3_first = shifted(v0[1], "y", 1), shifted(v0[0], "y", -1)
    v2 = shifted(v1_first, "y", 1), shifted(v3_rest, "y", -1)
    other_across = shifted(across, "core", 1)
    all_tokens = [own, ahead, across, behind, *other_near[:2], other_across, other_near[2]]
    outs = lax.all_gather(outs_four, "z")
    v1, v3 = (v1_first, v1_rest), (v3_first, v3_rest)
    place = jnp.stack([lax.axis_index(a) for a in ("z", "y", "x", "core")]).astype(jnp.int32)

    anywhere = pl.BlockSpec(memory_space=pl.ANY)
    smem = pl.BlockSpec(memory_space=pltpu.SMEM)
    vmem = pl.BlockSpec(memory_space=pltpu.VMEM)
    place = jnp.stack([lax.axis_index(a) for a in ("z", "y", "x", "core")]).astype(jnp.int32)

    anywhere = pl.BlockSpec(memory_space=pl.ANY)
    smem = pl.BlockSpec(memory_space=pltpu.SMEM)
    vmem = pl.BlockSpec(memory_space=pltpu.VMEM)
    value_part = pl.pallas_call(
        raw_kernel,
        in_specs=[smem] + [anywhere] * 14,
        out_specs=vmem,
        scratch_shapes=[
            pltpu.VMEM((8, rows + HALO, depth), BF16),
            pltpu.VMEM((8, depth, value), BF16),
            pltpu.SemaphoreType.DMA((8,)),
            pltpu.SemaphoreType.DMA((8, 4)),
        ],
        out_shape=jax.ShapeDtypeStruct((rows + HALO, value), F32),
        compiler_params=params(58),
        cost_estimate=cost(2 * rows * 8 * depth * value, 12 * rows * depth * 2),
        name="raw",
    )(place, *all_tokens, *v0, *v1, *v3)
    g0 = after(g0, *v2, value_part)
    g1, g3 = shifted(g0, "y", 1), shifted(g0, "y", -1)
    convolved, packed = pl.pallas_call(
        conv_kernel,
        in_specs=[smem] + [anywhere] * 11 + [vmem] * 5,
        out_specs=[vmem] * 2,
        scratch_shapes=[
            pltpu.VMEM((8, rows + HALO, depth), BF16),
            pltpu.VMEM((8, depth, keys), BF16),
            pltpu.VMEM((8 * depth // 4, value), BF16),
            pltpu.VMEM((rows + HALO, value + keys), F32),
            pltpu.SemaphoreType.DMA((8,)),
            pltpu.SemaphoreType.DMA((8,)),
            pltpu.SemaphoreType.DMA((8,)),
        ],
        out_shape=[
            jax.ShapeDtypeStruct((rows, value + keys), BF16),
            jax.ShapeDtypeStruct((pieces, N // pieces + 4, value), BF16),
        ],
        compiler_params=params(58),
        name="conv",
    )(
        place, *all_tokens, *v2, keys_all, value_part,
        conv_value, key_filter_taps, step, rate,
    )

    slices = lax.all_to_all(packed, CONTEXT, 0, 0, tiled=True)
    g1, g3, _ = after((g1, g3, packed))
    g2 = shifted(g1[:4], "y", 1), shifted(g3[4:], "y", -1)
    output = pl.pallas_call(
        scan_kernel,
        out_shape=jax.ShapeDtypeStruct((rows, value), F32),
        compiler_params=params(58),
        name="scan",
    )(convolved, step, rate, skip[:, None])

    starts = pl.pallas_call(
        prefix_kernel,
        in_specs=[vmem, anywhere],
        out_specs=vmem,
        out_shape=jax.ShapeDtypeStruct((pieces, N // pieces, value), BF16),
        compiler_params=params(58),
        name="prefix",
    )(slices, output)
    start = lax.all_to_all(starts, CONTEXT, 0, 0, tiled=True)

    gate = pl.pallas_call(
        gate_kernel,
        in_specs=[smem] + [anywhere] * 13,
        out_specs=vmem,
        scratch_shapes=[
            pltpu.VMEM((8, rows, depth), BF16),
            pltpu.VMEM((8, depth, value), BF16),
            pltpu.VMEM((rows, value), F32),
            pltpu.SemaphoreType.DMA((8,)),
            pltpu.SemaphoreType.DMA((8, 4)),
        ],
        out_shape=jax.ShapeDtypeStruct((rows, value), BF16),
        compiler_params=params(58),
        name="gate",
    )(place, *all_tokens, g0, g1, *g2, g3)

    normed = pl.pallas_call(
        norm_kernel,
        out_shape=jax.ShapeDtypeStruct((rows, value), BF16),
        compiler_params=params(58),
        name="norm",
    )(output, convolved, step, rate, start, gate, norm_gain[None, :])

    x, core = lax.axis_index("x"), lax.axis_index("core")

    half = rows // 2
    sibling = shifted(normed, "core", 1)

    def terms(earlier, distances, *kinds):
        count = len(distances)
        goals = [(x + d) % 4 * 2 + c for c in (core, 1 - core) for d in distances]
        block = (1, depth, value)
        return pl.pallas_call(
            out_kernel,
            grid_spec=pltpu.PrefetchScalarGridSpec(
                num_scalar_prefetch=1,
                grid=(count,),
                in_specs=[
                    pl.BlockSpec((rows, value), lambda j, t: (0, 0)),
                    pl.BlockSpec((rows, value), lambda j, t: (0, 0)),
                    pl.BlockSpec(block, lambda j, t: (t[j], 0, 0)),
                    pl.BlockSpec(block, lambda j, t: (t[count + j], 0, 0)),
                    anywhere,
                ],
                out_specs=[pl.BlockSpec((half, depth), lambda j, t: (0, 0))] * (2 * count),
            ),
            out_shape=[jax.ShapeDtypeStruct((half, depth), kind) for kind in kinds],
            compiler_params=params(58),
            cost_estimate=cost(8 * count * half * depth * value, 4 * count * depth * value),
            name="out",
        )(jnp.stack(goals).astype(jnp.int32), normed, sibling, outs, outs, earlier)

    far_upper, far_lower = terms(normed, (2,), BF16, BF16)
    from_behind = shifted(far_upper, "x", -1)
    from_ahead = shifted(far_lower, "x", 1)
    upper_ahead, lower_ahead, upper_behind, lower_behind = terms(
        far_upper, (1, 3), F32, BF16, BF16, F32
    )
    lower = shifted(lower_ahead, "x", -1)
    upper = shifted(upper_behind, "x", 1)
    upper_ahead = (upper_ahead + from_behind.astype(F32)).astype(BF16)
    lower_behind = (lower_behind + from_ahead.astype(F32)).astype(BF16)
    here_upper, here_lower = terms(upper_ahead, (0,), F32, F32)
    upper = here_upper + upper.astype(F32) + shifted(upper_ahead, "x", -1).astype(F32)
    lower = here_lower + lower.astype(F32) + shifted(lower_behind, "x", 1).astype(F32)
    return jnp.concatenate([upper, lower], axis=0).astype(BF16)


def solution(mesh):
    fine = Mesh(mesh.devices.reshape(8, 4, 4, 2), ("z", "y", "x", "core"))
    return jax.shard_map(
        local,
        mesh=fine,
        in_specs=(
            P(CONTEXT, TENSOR),
            P(CONTEXT, TENSOR),
            P(CONTEXT, TENSOR),
            P(CONTEXT, TENSOR),
            P(None, TENSOR),
            P(None, TENSOR),
            P(CONTEXT, TENSOR),
            P(TENSOR),
            P(TENSOR),
            P(TENSOR),
            P(TENSOR, CONTEXT),
        ),
        out_specs=P(CONTEXT, TENSOR),
        check_vma=False,
    )
```

time: 244 us -> 234 us (0.959)
  the two profiles are of different devices: /device:TPU:14 before, /device:TPU:1 now
where the time goes in v3:
time: 234 us; the launch traced here: 229 us
  starting transfers between devices  73 us (31%)
  waiting for transfers between devices  63.4 us (27%)
  Pallas kernels  55.2 us (24%)
  local copies, waits for them, and re-layouts  14.7 us (6%)
  between operations  13.8 us (6%)
  other arithmetic  9.23 us (4%)
    ppermute x31, waiting for transfers between devices, shifted(): lax.ppermute(array, axis, [((i + distance) % size, i) for i in range(size)])  54 us
    ppermute x31, starting transfers between devices, shifted(): lax.ppermute(array, axis, [((i + distance) % size, i) for i in range(size)])  33.6 us
    all_to_all x1, starting transfers between devices, local(): slices = lax.all_to_all(packed, CONTEXT, 0, 0, tiled=True)  21.1 us
    pallas_call x3, Pallas kernels, terms(): pl.pallas_call(out_kernel, grid_spec=pltpu.PrefetchScalarGridSpec(num_sca...  14.6 us
    pallas_call x1, Pallas kernels, local(): pl.pallas_call(conv_kernel, in_specs=[smem] + [anywhere] * 11 + [vmem] *...  12.4 us
    ppermute x1, starting transfers between devices, local(): swapped = lax.ppermute(after(w_out, keys_four), ('z', 'core'), swap)  11.6 us
    pallas_call x1, Pallas kernels, local(): pl.pallas_call(raw_kernel, in_specs=[smem] + [anywhere] * 14, out_specs=v...  7.78 us
    pallas_call x1, Pallas kernels, local(): pl.pallas_call(gate_kernel, in_specs=[smem] + [anywhere] * 13, out_specs=...  7.5 us
  transfers between devices with their start and end apart: 38, of which 18 were waited for; matrix products, arithmetic and copies ran while one was open for 7% of the time, Pallas kernels for 22%

profile of v3, /device:TPU:1, one launch (start us, length us, event | category | flops | bytes accessed | tf_op | source)
XLA Modules:
  0.0 229.3 jit_solution(15255811080521969676)
XLA Ops:
  6.5 1.8 pad_maximum_fusion.2
  8.4 3.6 %collective-permute-start.5 = (bf16[128,256]{1,0:T(8,128)(2,1)}, bf16[128,256]{1,0:T(8,128)(2,1)S(1)}, u32[]{:S(2)}, u32[]{:S(2)}) collective-permute-start(bf16[128,256]{1,0:T(8,128)(2,1)} %param.14), channel_id=1, source_target_pairs={{8,0},{16,8},{24,16},{0,24},{9,1},{17,9},{25,17},{1,25},{10,2},{18... | collective-permute-start | bytes 196616 | tf_op jit(solution)/shard_map/ppermute | solution.py:275
  14.0 3.0 %collective-permute-done.6 = bf16[128,256]{1,0:T(8,128)(2,1)S(1)} collective-permute-done((bf16[128,256]{1,0:T(8,128)(2,1)}, bf16[128,256]{1,0:T(8,128)(2,1)S(1)}, u32[]{:S(2)}, u32[]{:S(2)}) %collective-permute-start.6) | collective-permute-done | bytes 65568 | tf_op jit(solution)/shard_map/ppermute | solution.py:275
  21.5 2.6 %collective-permute-start.1 = (bf16[784,512]{1,0:T(8,128)(2,1)S(1)}, bf16[784,512]{1,0:T(8,128)(2,1)S(1)}, u32[]{:S(2)}, u32[]{:S(2)}) collective-permute-start(bf16[784,512]{1,0:T(8,128)(2,1)S(1)} %constant_dynamic-update-slice_fusion.refs_0_), channel_id=1, source_target_pairs={{2,0},{4,2},{6,4},{0,6},{3,1},{5,3},{7,5},{1,7},{10,8},{12,10},{14... | collective-permute-start | bytes 2408456 | tf_op jit(solution)/shard_map/ppermute | solution.py:275
  24.0 11.6 %collective-permute-start.8 = (bf16[512,128]{1,0:T(8,128)(2,1)S(1)}, bf16[512,128]{1,0:T(8,128)(2,1)S(1)}, u32[]{:S(2)}, u32[]{:S(2)}) collective-permute-start(bf16[512,128]{1,0:T(8,128)(2,1)S(1)} %copy-done.19), channel_id=1, source_target_pairs={{0,0},{1,32},{32,1},{33,33},{64,64},{65,96},{96,65},{97,97},{128,1... | collective-permute-start | bytes 393224 | tf_op jit(solution)/shard_map/ppermute | solution.py:313
  35.6 4.6 %collective-permute-done.8 = bf16[512,128]{1,0:T(8,128)(2,1)S(1)} collective-permute-done((bf16[512,128]{1,0:T(8,128)(2,1)S(1)}, bf16[512,128]{1,0:T(8,128)(2,1)S(1)}, u32[]{:S(2)}, u32[]{:S(2)}) %collective-permute-start.8) | collective-permute-done | bytes 131104 | tf_op jit(solution)/shard_map/ppermute | solution.py:313
  40.8 4.4 %collective-permute-done.9 = bf16[512,128]{1,0:T(8,128)(2,1)S(1)} collective-permute-done((bf16[512,128]{1,0:T(8,128)(2,1)S(1)}, bf16[512,128]{1,0:T(8,128)(2,1)S(1)}, u32[]{:S(2)}, u32[]{:S(2)}) %collective-permute-start.9) | collective-permute-done | bytes 131104 | tf_op jit(solution)/shard_map/ppermute | solution.py:275
  45.2 1.6 collective-permute-done.10
  46.9 1.6 collective-permute-start.13
  48.6 2.1 collective-permute-done.11
  50.8 4.2 %collective-permute-start.3 = (bf16[400,512]{1,0:T(8,128)(2,1)S(1)}, bf16[400,512]{1,0:T(8,128)(2,1)}, u32[]{:S(2)}, u32[]{:S(2)}) collective-permute-start(bf16[400,512]{1,0:T(8,128)(2,1)S(1)} %slice.32), channel_id=1, source_target_pairs={{2,0},{4,2},{6,4},{0,6},{3,1},{5,3},{7,5},{1,7},{10,8},{12,10},{14... | collective-permute-start | bytes 1228808 | tf_op jit(solution)/shard_map/ppermute | solution.py:275
  56.2 9.9 %collective-permute-done.4 = bf16[384,512]{1,0:T(8,128)(2,1)} collective-permute-done((bf16[384,512]{1,0:T(8,128)(2,1)S(1)}, bf16[384,512]{1,0:T(8,128)(2,1)}, u32[]{:S(2)}, u32[]{:S(2)}) %collective-permute-start.4) | collective-permute-done | bytes 393248 | tf_op jit(solution)/shard_map/ppermute | solution.py:275
  67.4 2.3 %fusion = (bf16[4,128,512]{2,1,0:T(8,128)(2,1)}, bf16[4,128,512]{2,1,0:T(8,128)(2,1)}) fusion(bf16[8,128,1024]{2,1,0:T(8,128)(2,1)} %bitcast.24), kind=kLoop, calls=%fused_computation.31 | loop fusion | bytes 2097152 | tf_op jit(solution)/shard_map/slice | solution.py:328
  73.0 10.2 %collective-permute-done.16.refs_10_ = bf16[4,128,512]{2,1,0:T(8,128)(2,1)} collective-permute-done((bf16[4,128,512]{2,1,0:T(8,128)(2,1)}, bf16[4,128,512]{2,1,0:T(8,128)(2,1)}, u32[]{:S(2)}, u32[]{:S(2)}) %collective-permute-start.16) | collective-permute-done | bytes 524320 | tf_op jit(solution)/shard_map/ppermute | solution.py:275
  86.7 7.7 %collective-permute-done.20.refs_11_ = bf16[4,128,512]{2,1,0:T(8,128)(2,1)} collective-permute-done((bf16[4,128,512]{2,1,0:T(8,128)(2,1)}, bf16[4,128,512]{2,1,0:T(8,128)(2,1)}, u32[]{:S(2)}, u32[]{:S(2)}) %collective-permute-start.20) | collective-permute-done | bytes 524320 | tf_op jit(solution)/shard_map/ppermute | solution.py:275
  96.8 7.8 %raw.1.refs_11_ = f32[784,512]{1,0:T(8,128)} custom-call(s32[4]{0:T(128)} %pad_add_fusion.1.place, bf16[784,512]{1,0:T(8,128)(2,1)} %copy-done.5, bf16[784,512]{1,0:T(8,128)(2,1)} %copy-done.2, bf16[784,512]{1,0:T(8,128)(2,1)} %copy-done, bf16[784,512]{1,0:T(8,128)(2,1)} %copy-done.3, bf16[784,512]{1,0:T(8,128)(2,1)} %collective-permute-done.12.refs_4_, ...), custom_call_target="tpu_custom_call" | custom-call | flops 3221225472 | bytes 9437184 | tf_op jit(solution)/shard_map/raw/pallas_call | solution.py:347
  109.3 12.4 %conv.1 = (bf16[768,768]{1,0:T(8,128)(2,1)}, bf16[32,8,512]{2,1,0:T(8,128)(2,1)}) custom-call(s32[4]{0:T(128)} %pad_add_fusion.1.place, bf16[784,512]{1,0:T(8,128)(2,1)} %copy-done.5, bf16[784,512]{1,0:T(8,128)(2,1)} %copy-done.2, bf16[784,512]{1,0:T(8,128)(2,1)} %copy-done, bf16[784,512]{1,0:T(8,128)(2,1)} %copy-done.3, ...), custom_call_target="tpu_custom_call" | custom-call | tf_op jit(solution)/shard_map/conv/pallas_call | solution.py:364
  121.7 21.1 %all-to-all-start = ((bf16[32,8,512]{2,1,0:T(8,128)(2,1)}), bf16[32,8,512]{2,1,0:T(8,128)(2,1)S(1)}, u32[]{:S(2)}, u32[]{:S(2)}) async-start(bf16[32,8,512]{2,1,0:T(8,128)(2,1)} %get-tuple-element.36), calls=%async_computation | async-start | bytes 524288 | tf_op jit(solution)/shard_map/all_to_all | solution.py:388
  142.9 2.4 %collective-permute-start.24 = (bf16[4,128,512]{2,1,0:T(8,128)(2,1)S(1)}, bf16[4,128,512]{2,1,0:T(8,128)(2,1)S(1)}, u32[]{:S(2)}, u32[]{:S(2)}) collective-permute-start(bf16[4,128,512]{2,1,0:T(8,128)(2,1)S(1)} %slice.30), channel_id=1, source_target_pairs={{8,0},{16,8},{24,16},{0,24},{9,1},{17,9},{25,17},{1,25},{10,2},{18... | collective-permute-start | bytes 1572872 | tf_op jit(solution)/shard_map/ppermute | solution.py:275
  147.2 6.2 %scan.1.earlier.output = f32[768,512]{1,0:T(8,128)} custom-call(bf16[768,768]{1,0:T(8,128)(2,1)} %get-tuple-element.35.conv, f32[8,768]{1,0:T(8,128)} %bitcast.27, f32[8,1]{1,0:T(8,128)} %copy.12.refs_15_.rate, f32[8,1]{1,0:T(8,128)} %copy.14.skip), custom_call_target="tpu_custom_call" | custom-call | tf_op jit(solution)/shard_map/scan/pallas_call | solution.py:391
  153.3 3.7 %all-to-all-done.states = bf16[32,8,512]{2,1,0:T(8,128)(2,1)S(1)} async-done(((bf16[32,8,512]{2,1,0:T(8,128)(2,1)}), bf16[32,8,512]{2,1,0:T(8,128)(2,1)S(1)}, u32[]{:S(2)}, u32[]{:S(2)}) %all-to-all-start) | async-done | bytes 262176 | tf_op jit(solution)/shard_map/all_to_all | solution.py:388
  157.8 1.8 prefix.1
  159.6 5.4 %all-to-all-start.1 = ((bf16[32,4,512]{2,1,0:T(4,128)(2,1)}), bf16[32,4,512]{2,1,0:T(4,128)(2,1)S(1)}, u32[]{:S(2)}, u32[]{:S(2)}) async-start(bf16[32,4,512]{2,1,0:T(4,128)(2,1)} %prefix.1), calls=%async_computation.1 | async-start | bytes 262144 | tf_op jit(solution)/shard_map/all_to_all | solution.py:406
  166.7 7.5 %gate.1 = bf16[768,512]{1,0:T(8,128)(2,1)} custom-call(s32[4]{0:T(128)} %pad_add_fusion.1.place, bf16[784,512]{1,0:T(8,128)(2,1)} %copy-done.5, bf16[784,512]{1,0:T(8,128)(2,1)} %copy-done.2, bf16[784,512]{1,0:T(8,128)(2,1)} %copy-done, bf16[784,512]{1,0:T(8,128)(2,1)} %copy-done.3, bf16[784,512]{1,0:T(8,128)(2,1)} %collective-permute-done.12.refs_4_, ...), custom_call_target="tpu_custom_call" | custom-call | tf_op jit(solution)/shard_map/gate/pallas_call | solution.py:408
  175.0 4.9 %norm.1.own.earlier = bf16[768,512]{1,0:T(8,128)(2,1)} custom-call(f32[768,512]{1,0:T(8,128)} %scan.1.earlier.output, bf16[768,768]{1,0:T(8,128)(2,1)} %get-tuple-element.35.conv, f32[8,768]{1,0:T(8,128)} %bitcast.28, f32[8,1]{1,0:T(8,128)} %copy.12.refs_15_.rate, bf16[32,4,512]{2,1,0:T(4,128)(2,1)} %copy-done.16, bf16[768,512]{1,0:T(8,128)(2,1)} %gate.1, ...), custom_call_target="tpu_custom_call" | custom-call | tf_op jit(solution)/shard_map/norm/pallas_call | solution.py:424
  179.8 4.0 %collective-permute-start.26 = (bf16[768,512]{1,0:T(8,128)(2,1)}, bf16[768,512]{1,0:T(8,128)(2,1)S(1)}, u32[]{:S(2)}, u32[]{:S(2)}) collective-permute-start(bf16[768,512]{1,0:T(8,128)(2,1)} %norm.1.own.earlier), channel_id=1, source_target_pairs={{1,0},{0,1},{3,2},{2,3},{5,4},{4,5},{7,6},{6,7},{9,8},{8,9},{11,10... | collective-permute-start | bytes 2359304 | tf_op jit(solution)/shard_map/ppermute | solution.py:275
  186.8 4.1 %out.3 = (bf16[384,512]{1,0:T(8,128)(2,1)}, bf16[384,512]{1,0:T(8,128)(2,1)}) custom-call(s32[2]{0:T(128)} %pad_add_fusion.3.targets, bf16[768,512]{1,0:T(8,128)(2,1)} %norm.1.own.earlier, bf16[768,512]{1,0:T(8,128)(2,1)} %copy-done.1, bf16[8,512,512]{2,1,0:T(8,128)(2,1)} %bitcast.18, bf16[8,512,512]{2,1,0:T(8,128)(2,1)} %bitcast.19, ...), custom_call_target="tpu_custom_call" | custom-call | flops 805306368 | bytes 1048576 | tf_op jit(solution)/shard_map/out/pallas_call | solution.py:440
  191.5 2.7 %collective-permute-start.31 = (bf16[384,512]{1,0:T(8,128)(2,1)}, bf16[384,512]{1,0:T(8,128)(2,1)S(1)}, u32[]{:S(2)}, u32[]{:S(2)}) collective-permute-start(bf16[384,512]{1,0:T(8,128)(2,1)} %get-tuple-element.48), channel_id=1, source_target_pairs={{2,0},{4,2},{6,4},{0,6},{3,1},{5,3},{7,5},{1,7},{10,8},{12,10},{14... | collective-permute-start | bytes 1179656 | tf_op jit(solution)/shard_map/ppermute | solution.py:275
  194.2 6.3 %out.4 = (f32[384,512]{1,0:T(8,128)}, bf16[384,512]{1,0:T(8,128)(2,1)}, bf16[384,512]{1,0:T(8,128)(2,1)}, f32[384,512]{1,0:T(8,128)}) custom-call(s32[4]{0:T(128)} %pad_add_fusion.2.targets, bf16[768,512]{1,0:T(8,128)(2,1)} %norm.1.own.earlier, bf16[768,512]{1,0:T(8,128)(2,1)} %copy-done.1, bf16[8,512,512]{2,1,0:T(8,128)(2,1)} %bitcast.20, ...), custom_call_target="tpu_custom_call" | custom-call | flops 1610612736 | bytes 2097152 | tf_op jit(solution)/shard_map/out/pallas_call | solution.py:440
  204.1 2.7 %collective-permute-start.32 = (bf16[384,512]{1,0:T(8,128)(2,1)S(1)}, bf16[384,512]{1,0:T(8,128)(2,1)S(1)}, u32[]{:S(2)}, u32[]{:S(2)}) collective-permute-start(bf16[384,512]{1,0:T(8,128)(2,1)S(1)} %add_convert_fusion.1), channel_id=1, source_target_pairs={{2,0},{4,2},{6,4},{0,6},{3,1},{5,3},{7,5},{1,7},{10,8},{12,10},{14... | collective-permute-start | bytes 1179656 | tf_op jit(solution)/shard_map/ppermute | solution.py:275
  207.5 4.2 %out.5 = (f32[384,512]{1,0:T(8,128)}, f32[384,512]{1,0:T(8,128)}) custom-call(s32[2]{0:T(128)} %pad_add_fusion.targets, bf16[768,512]{1,0:T(8,128)(2,1)} %norm.1.own.earlier, bf16[768,512]{1,0:T(8,128)(2,1)} %copy-done.1, bf16[8,512,512]{2,1,0:T(8,128)(2,1)} %bitcast.22, bf16[8,512,512]{2,1,0:T(8,128)(2,1)} %bitcast.23, bf16[384,512]{1,0:T(8,128)(2,1)} %copy-done.8), custom_call_target="tpu_custom_call" | custom-call | flops 805306368 | bytes 1048576 | tf_op jit(solution)/shard_map/out/pallas_call | solution.py:440
  211.7 8.4 %collective-permute-done.29 = bf16[384,512]{1,0:T(8,128)(2,1)S(1)} collective-permute-done((bf16[384,512]{1,0:T(8,128)(2,1)S(1)}, bf16[384,512]{1,0:T(8,128)(2,1)S(1)}, u32[]{:S(2)}, u32[]{:S(2)}) %collective-permute-start.29) | collective-permute-done | bytes 393248 | tf_op jit(solution)/shard_map/ppermute | solution.py:275
  (136 shorter events, 38.8 us)
Async XLA Ops:
  6.5 60.8 %all-gather.8.cloned.1.call-start = ((), (), s32[]{:S(2)}) async-start(), calls=%async_computation.3 | async-start | bytes 2359296 | tf_op jit(solution)/shard_map/all_gather | solution.py:307
  8.3 101.0 %all-gather.6.cloned.1.call-start = ((), (), s32[]{:S(2)}) async-start(), calls=%async_computation.2 | async-start | bytes 2359296 | tf_op jit(solution)/shard_map/all_gather | solution.py:323
  19.2 166.8 %all-gather.10.cloned.1.call-start = ((), (), s32[]{:S(2)}) async-start(), calls=%async_computation.4 | async-start | bytes 4718592 | tf_op jit(solution)/shard_map/all_gather | solution.py:335
  21.5 25.4 %collective-permute-start.1 = (bf16[784,512]{1,0:T(8,128)(2,1)S(1)}, bf16[784,512]{1,0:T(8,128)(2,1)S(1)}, u32[]{:S(2)}, u32[]{:S(2)}) collective-permute-start(bf16[784,512]{1,0:T(8,128)(2,1)S(1)} %constant_dynamic-update-slice_fusion.refs_0_), channel_id=1, source_target_pairs={{2,0},{4,2},{6,4},{0,6},{3,1},{5,3},{7,5},{1,7},{10,8},{12,10},{14... | collective-permute-start | bytes 2408456 | tf_op jit(solution)/shard_map/ppermute | solution.py:275
  24.0 24.4 %collective-permute-start.2 = (bf16[784,512]{1,0:T(8,128)(2,1)S(1)}, bf16[784,512]{1,0:T(8,128)(2,1)S(1)}, u32[]{:S(2)}, u32[]{:S(2)}) collective-permute-start(bf16[784,512]{1,0:T(8,128)(2,1)S(1)} %constant_dynamic-update-slice_fusion.refs_0_), channel_id=1, source_target_pairs={{6,0},{0,2},{2,4},{4,6},{7,1},{1,3},{3,5},{5,7},{14,8},{8,10},{10,... | collective-permute-start | bytes 2408456 | tf_op jit(solution)/shard_map/ppermute | solution.py:275
  24.0 16.2 %collective-permute-start.8 = (bf16[512,128]{1,0:T(8,128)(2,1)S(1)}, bf16[512,128]{1,0:T(8,128)(2,1)S(1)}, u32[]{:S(2)}, u32[]{:S(2)}) collective-permute-start(bf16[512,128]{1,0:T(8,128)(2,1)S(1)} %copy-done.19), channel_id=1, source_target_pairs={{0,0},{1,32},{32,1},{33,33},{64,64},{65,96},{96,65},{97,97},{128,1... | collective-permute-start | bytes 393224 | tf_op jit(solution)/shard_map/ppermute | solution.py:313
  40.8 26.5 %collective-permute-start.12 = (bf16[784,512]{1,0:T(8,128)(2,1)S(1)}, bf16[784,512]{1,0:T(8,128)(2,1)}, u32[]{:S(2)}, u32[]{:S(2)}) collective-permute-start(bf16[784,512]{1,0:T(8,128)(2,1)S(1)} %constant_dynamic-update-slice_fusion.refs_0_), channel_id=1, source_target_pairs={{1,0},{0,1},{3,2},{2,3},{5,4},{4,5},{7,6},{6,7},{9,8},{8,9},{11,10... | collective-permute-start | bytes 2408456 | tf_op jit(solution)/shard_map/ppermute | solution.py:275
  40.8 6.1 %collective-permute-start.10 = (bf16[512,128]{1,0:T(8,128)(2,1)S(1)}, bf16[512,128]{1,0:T(8,128)(2,1)S(1)}, u32[]{:S(2)}, u32[]{:S(2)}) collective-permute-start(bf16[512,128]{1,0:T(8,128)(2,1)S(1)} %collective-permute-done.8), channel_id=1, source_target_pairs={{16,0},{24,8},{0,16},{8,24},{17,1},{25,9},{1,17},{9,25},{18,2},{26... | collective-permute-start | bytes 393224 | tf_op jit(solution)/shard_map/ppermute | solution.py:275
  46.9 20.4 %collective-permute-start.13 = (bf16[784,512]{1,0:T(8,128)(2,1)S(1)}, bf16[784,512]{1,0:T(8,128)(2,1)}, u32[]{:S(2)}, u32[]{:S(2)}) collective-permute-start(bf16[784,512]{1,0:T(8,128)(2,1)S(1)} %collective-permute-done.1.refs_1_), channel_id=1, source_target_pairs={{1,0},{0,1},{3,2},{2,3},{5,4},{4,5},{7,6},{6,7},{9,8},{8,9},{11,10... | collective-permute-start | bytes 2408456 | tf_op jit(solution)/shard_map/ppermute | solution.py:275
  48.4 18.8 %collective-permute-start.14 = (bf16[784,512]{1,0:T(8,128)(2,1)S(1)}, bf16[784,512]{1,0:T(8,128)(2,1)}, u32[]{:S(2)}, u32[]{:S(2)}) collective-permute-start(bf16[784,512]{1,0:T(8,128)(2,1)S(1)} %collective-permute-done.2.refs_3_), channel_id=1, source_target_pairs={{1,0},{0,1},{3,2},{2,3},{5,4},{4,5},{7,6},{6,7},{9,8},{8,9},{11,10... | collective-permute-start | bytes 2408456 | tf_op jit(solution)/shard_map/ppermute | solution.py:275
  50.8 15.2 %collective-permute-start.3 = (bf16[400,512]{1,0:T(8,128)(2,1)S(1)}, bf16[400,512]{1,0:T(8,128)(2,1)}, u32[]{:S(2)}, u32[]{:S(2)}) collective-permute-start(bf16[400,512]{1,0:T(8,128)(2,1)S(1)} %slice.32), channel_id=1, source_target_pairs={{2,0},{4,2},{6,4},{0,6},{3,1},{5,3},{7,5},{1,7},{10,8},{12,10},{14... | collective-permute-start | bytes 1228808 | tf_op jit(solution)/shard_map/ppermute | solution.py:275
  55.1 11.0 %collective-permute-start.4 = (bf16[384,512]{1,0:T(8,128)(2,1)S(1)}, bf16[384,512]{1,0:T(8,128)(2,1)}, u32[]{:S(2)}, u32[]{:S(2)}) collective-permute-start(bf16[384,512]{1,0:T(8,128)(2,1)S(1)} %slice.33), channel_id=1, source_target_pairs={{6,0},{0,2},{2,4},{4,6},{7,1},{1,3},{3,5},{5,7},{14,8},{8,10},{10,... | collective-permute-start | bytes 1179656 | tf_op jit(solution)/shard_map/ppermute | solution.py:275
  67.3 28.6 %collective-permute-start.15 = (bf16[784,512]{1,0:T(8,128)(2,1)S(1)}, bf16[784,512]{1,0:T(8,128)(2,1)S(1)}, u32[]{:S(2)}, u32[]{:S(2)}) collective-permute-start(bf16[784,512]{1,0:T(8,128)(2,1)S(1)} %pad_maximum_fusion.refs_2_), channel_id=1, source_target_pairs={{1,0},{0,1},{3,2},{2,3},{5,4},{4,5},{7,6},{6,7},{9,8},{8,9},{11,10... | collective-permute-start | bytes 2408456 | tf_op jit(solution)/shard_map/ppermute | solution.py:275
  69.8 13.4 %collective-permute-start.16 = (bf16[4,128,512]{2,1,0:T(8,128)(2,1)}, bf16[4,128,512]{2,1,0:T(8,128)(2,1)}, u32[]{:S(2)}, u32[]{:S(2)}) collective-permute-start(bf16[4,128,512]{2,1,0:T(8,128)(2,1)} %get-tuple-element.50.refs_8_), channel_id=1, source_target_pairs={{8,0},{16,8},{24,16},{0,24},{9,1},{17,9},{25,17},{1,25},{10,2},{18... | collective-permute-start | bytes 1572872 | tf_op jit(solution)/shard_map/ppermute | solution.py:275
  70.1 14.6 %collective-permute-start.18 = (bf16[4,128,512]{2,1,0:T(8,128)(2,1)}, bf16[4,128,512]{2,1,0:T(8,128)(2,1)}, u32[]{:S(2)}, u32[]{:S(2)}) collective-permute-start(bf16[4,128,512]{2,1,0:T(8,128)(2,1)} %get-tuple-element.49.refs_9_), channel_id=1, source_target_pairs={{24,0},{0,8},{8,16},{16,24},{25,1},{1,9},{9,17},{17,25},{26,2},{2,... | collective-permute-start | bytes 1572872 | tf_op jit(solution)/shard_map/ppermute | solution.py:275
  71.5 23.0 %collective-permute-start.20 = (bf16[4,128,512]{2,1,0:T(8,128)(2,1)}, bf16[4,128,512]{2,1,0:T(8,128)(2,1)}, u32[]{:S(2)}, u32[]{:S(2)}) collective-permute-start(bf16[4,128,512]{2,1,0:T(8,128)(2,1)} %get-tuple-element.49.refs_9_), channel_id=1, source_target_pairs={{8,0},{16,8},{24,16},{0,24},{9,1},{17,9},{25,17},{1,25},{10,2},{18... | collective-permute-start | bytes 1572872 | tf_op jit(solution)/shard_map/ppermute | solution.py:275
  73.0 22.9 %collective-permute-start.21 = (bf16[4,128,512]{2,1,0:T(8,128)(2,1)}, bf16[4,128,512]{2,1,0:T(8,128)(2,1)}, u32[]{:S(2)}, u32[]{:S(2)}) collective-permute-start(bf16[4,128,512]{2,1,0:T(8,128)(2,1)} %get-tuple-element.50.refs_8_), channel_id=1, source_target_pairs={{24,0},{0,8},{8,16},{16,24},{25,1},{1,9},{9,17},{17,25},{26,2},{2,... | collective-permute-start | bytes 1572872 | tf_op jit(solution)/shard_map/ppermute | solution.py:275
  83.2 22.5 %collective-permute-start.17 = (bf16[4,128,512]{2,1,0:T(8,128)(2,1)}, bf16[4,128,512]{2,1,0:T(8,128)(2,1)S(1)}, u32[]{:S(2)}, u32[]{:S(2)}) collective-permute-start(bf16[4,128,512]{2,1,0:T(8,128)(2,1)} %collective-permute-done.16.refs_10_), channel_id=1, source_target_pairs={{8,0},{16,8},{24,16},{0,24},{9,1},{17,9},{25,17},{1,25},{10,2},{18... | collective-permute-start | bytes 1572872 | tf_op jit(solution)/shard_map/ppermute | solution.py:275
  84.8 22.4 %collective-permute-start.19 = (bf16[4,128,512]{2,1,0:T(8,128)(2,1)}, bf16[4,128,512]{2,1,0:T(8,128)(2,1)}, u32[]{:S(2)}, u32[]{:S(2)}) collective-permute-start(bf16[4,128,512]{2,1,0:T(8,128)(2,1)} %collective-permute-done.18.refs_13_), channel_id=1, source_target_pairs={{24,0},{0,8},{8,16},{16,24},{25,1},{1,9},{9,17},{17,25},{26,2},{2,... | collective-permute-start | bytes 1572872 | tf_op jit(solution)/shard_map/ppermute | solution.py:275
  107.1 35.7 %collective-permute-start.22 = (bf16[8,128,512]{2,1,0:T(8,128)(2,1)S(1)}, bf16[8,128,512]{2,1,0:T(8,128)(2,1)S(1)}, u32[]{:S(2)}, u32[]{:S(2)}) collective-permute-start(bf16[8,128,512]{2,1,0:T(8,128)(2,1)S(1)} %slice.29.refs_8_), channel_id=1, source_target_pairs={{8,0},{16,8},{24,16},{0,24},{9,1},{17,9},{25,17},{1,25},{10,2},{18... | collective-permute-start | bytes 3145736 | tf_op jit(solution)/shard_map/ppermute | solution.py:275
  107.9 35.0 %collective-permute-start.23 = (bf16[8,128,512]{2,1,0:T(8,128)(2,1)S(1)}, bf16[8,128,512]{2,1,0:T(8,128)(2,1)}, u32[]{:S(2)}, u32[]{:S(2)}) collective-permute-start(bf16[8,128,512]{2,1,0:T(8,128)(2,1)S(1)} %slice.29.refs_8_), channel_id=1, source_target_pairs={{24,0},{0,8},{8,16},{16,24},{25,1},{1,9},{9,17},{17,25},{26,2},{2,... | collective-permute-start | bytes 3145736 | tf_op jit(solution)/shard_map/ppermute | solution.py:275
  121.7 35.3 %all-to-all-start = ((bf16[32,8,512]{2,1,0:T(8,128)(2,1)}), bf16[32,8,512]{2,1,0:T(8,128)(2,1)S(1)}, u32[]{:S(2)}, u32[]{:S(2)}) async-start(bf16[32,8,512]{2,1,0:T(8,128)(2,1)} %get-tuple-element.36), calls=%async_computation | async-start | bytes 524288 | tf_op jit(solution)/shard_map/all_to_all | solution.py:388
  142.9 22.1 %collective-permute-start.24 = (bf16[4,128,512]{2,1,0:T(8,128)(2,1)S(1)}, bf16[4,128,512]{2,1,0:T(8,128)(2,1)S(1)}, u32[]{:S(2)}, u32[]{:S(2)}) collective-permute-start(bf16[4,128,512]{2,1,0:T(8,128)(2,1)S(1)} %slice.30), channel_id=1, source_target_pairs={{8,0},{16,8},{24,16},{0,24},{9,1},{17,9},{25,17},{1,25},{10,2},{18... | collective-permute-start | bytes 1572872 | tf_op jit(solution)/shard_map/ppermute | solution.py:275
  146.4 18.6 %collective-permute-start.25 = (bf16[4,128,512]{2,1,0:T(8,128)(2,1)S(1)}, bf16[4,128,512]{2,1,0:T(8,128)(2,1)S(1)}, u32[]{:S(2)}, u32[]{:S(2)}) collective-permute-start(bf16[4,128,512]{2,1,0:T(8,128)(2,1)S(1)} %slice.31), channel_id=1, source_target_pairs={{24,0},{0,8},{8,16},{16,24},{25,1},{1,9},{9,17},{17,25},{26,2},{2,... | collective-permute-start | bytes 1572872 | tf_op jit(solution)/shard_map/ppermute | solution.py:275
  159.6 14.8 %all-to-all-start.1 = ((bf16[32,4,512]{2,1,0:T(4,128)(2,1)}), bf16[32,4,512]{2,1,0:T(4,128)(2,1)S(1)}, u32[]{:S(2)}, u32[]{:S(2)}) async-start(bf16[32,4,512]{2,1,0:T(4,128)(2,1)} %prefix.1), calls=%async_computation.1 | async-start | bytes 262144 | tf_op jit(solution)/shard_map/all_to_all | solution.py:406
  179.8 6.1 %collective-permute-start.26 = (bf16[768,512]{1,0:T(8,128)(2,1)}, bf16[768,512]{1,0:T(8,128)(2,1)S(1)}, u32[]{:S(2)}, u32[]{:S(2)}) collective-permute-start(bf16[768,512]{1,0:T(8,128)(2,1)} %norm.1.own.earlier), channel_id=1, source_target_pairs={{1,0},{0,1},{3,2},{2,3},{5,4},{4,5},{7,6},{6,7},{9,8},{8,9},{11,10... | collective-permute-start | bytes 2359304 | tf_op jit(solution)/shard_map/ppermute | solution.py:275
  190.9 11.8 %collective-permute-start.27 = (bf16[384,512]{1,0:T(8,128)(2,1)}, bf16[384,512]{1,0:T(8,128)(2,1)S(1)}, u32[]{:S(2)}, u32[]{:S(2)}) collective-permute-start(bf16[384,512]{1,0:T(8,128)(2,1)} %get-tuple-element.41.earlier), channel_id=1, source_target_pairs={{6,0},{0,2},{2,4},{4,6},{7,1},{1,3},{3,5},{5,7},{14,8},{8,10},{10,... | collective-permute-start | bytes 1179656 | tf_op jit(solution)/shard_map/ppermute | solution.py:275
  191.5 12.5 %collective-permute-start.31 = (bf16[384,512]{1,0:T(8,128)(2,1)}, bf16[384,512]{1,0:T(8,128)(2,1)S(1)}, u32[]{:S(2)}, u32[]{:S(2)}) collective-permute-start(bf16[384,512]{1,0:T(8,128)(2,1)} %get-tuple-element.48), channel_id=1, source_target_pairs={{2,0},{4,2},{6,4},{0,6},{3,1},{5,3},{7,5},{1,7},{10,8},{12,10},{14... | collective-permute-start | bytes 1179656 | tf_op jit(solution)/shard_map/ppermute | solution.py:275
  200.5 11.2 %collective-permute-start.28 = (bf16[384,512]{1,0:T(8,128)(2,1)}, bf16[384,512]{1,0:T(8,128)(2,1)S(1)}, u32[]{:S(2)}, u32[]{:S(2)}) collective-permute-start(bf16[384,512]{1,0:T(8,128)(2,1)} %get-tuple-element.44), channel_id=1, source_target_pairs={{2,0},{4,2},{6,4},{0,6},{3,1},{5,3},{7,5},{1,7},{10,8},{12,10},{14... | collective-permute-start | bytes 1179656 | tf_op jit(solution)/shard_map/ppermute | solution.py:275
  200.5 20.9 %collective-permute-start.30 = (bf16[384,512]{1,0:T(8,128)(2,1)}, bf16[384,512]{1,0:T(8,128)(2,1)S(1)}, u32[]{:S(2)}, u32[]{:S(2)}) collective-permute-start(bf16[384,512]{1,0:T(8,128)(2,1)} %get-tuple-element.46), channel_id=1, source_target_pairs={{6,0},{0,2},{2,4},{4,6},{7,1},{1,3},{3,5},{5,7},{14,8},{8,10},{10,... | collective-permute-start | bytes 1179656 | tf_op jit(solution)/shard_map/ppermute | solution.py:275
  203.9 16.2 %collective-permute-start.29 = (bf16[384,512]{1,0:T(8,128)(2,1)S(1)}, bf16[384,512]{1,0:T(8,128)(2,1)S(1)}, u32[]{:S(2)}, u32[]{:S(2)}) collective-permute-start(bf16[384,512]{1,0:T(8,128)(2,1)S(1)} %add_convert_fusion.3.earlier), channel_id=1, source_target_pairs={{6,0},{0,2},{2,4},{4,6},{7,1},{1,3},{3,5},{5,7},{14,8},{8,10},{10,... | collective-permute-start | bytes 1179656 | tf_op jit(solution)/shard_map/ppermute | solution.py:275
  204.1 17.3 %collective-permute-start.32 = (bf16[384,512]{1,0:T(8,128)(2,1)S(1)}, bf16[384,512]{1,0:T(8,128)(2,1)S(1)}, u32[]{:S(2)}, u32[]{:S(2)}) collective-permute-start(bf16[384,512]{1,0:T(8,128)(2,1)S(1)} %add_convert_fusion.1), channel_id=1, source_target_pairs={{2,0},{4,2},{6,4},{0,6},{3,1},{5,3},{7,5},{1,7},{10,8},{12,10},{14... | collective-permute-start | bytes 1179656 | tf_op jit(solution)/shard_map/ppermute | solution.py:275
  (26 other events, 225.0 us)
Sparse Core Ops, SparseCore 0:
  9.1 41.9 all-gather.7
  52.9 39.4 all-gather.5
  94.2 62.2 all-gather.9

commit v4 on v3

--- a/solution.py
+++ b/solution.py
@@ -326,9 +326,9 @@
         (both, ahead, behind, across, outs_four, *other_near)
     )
     v0 = both[:4, :, :value], both[4:, :, :value]
-    g0 = both[..., value:]
     v1_first, v3_rest = shifted(v0[0], "y", 1), shifted(v0[1], "y", -1)
     v1_rest, v3_first = shifted(v0[1], "y", 1), shifted(v0[0], "y", -1)
+    g0 = after(both, v1_first)[..., value:]
     v2 = shifted(v1_first, "y", 1), shifted(v3_rest, "y", -1)
     other_across = shifted(across, "core", 1)
     all_tokens = [own, ahead, across, behind, *other_near[:2], other_across, other_near[2]]

time: 234 us -> 234 us (level)
  no operation moved by 1% of the time
where the time goes in v4:
time: 234 us; the launch traced here: 229 us
  starting transfers between devices  73 us (31%)
  waiting for transfers between devices  63.4 us (27%)
  Pallas kernels  55.2 us (24%)
  local copies, waits for them, and re-layouts  14.7 us (6%)
  between operations  13.8 us (6%)
  other arithmetic  9.23 us (4%)
    ppermute x31, waiting for transfers between devices, shifted(): lax.ppermute(array, axis, [((i + distance) % size, i) for i in range(size)])  54 us
    ppermute x31, starting transfers between devices, shifted(): lax.ppermute(array, axis, [((i + distance) % size, i) for i in range(size)])  33.6 us
    all_to_all x1, starting transfers between devices, local(): slices = lax.all_to_all(packed, CONTEXT, 0, 0, tiled=True)  21.1 us
    pallas_call x3, Pallas kernels, terms(): pl.pallas_call(out_kernel, grid_spec=pltpu.PrefetchScalarGridSpec(num_sca...  14.6 us
    pallas_call x1, Pallas kernels, local(): pl.pallas_call(conv_kernel, in_specs=[smem] + [anywhere] * 11 + [vmem] *...  12.4 us
    ppermute x1, starting transfers between devices, local(): swapped = lax.ppermute(after(w_out, keys_four), ('z', 'core'), swap)  11.6 us
    pallas_call x1, Pallas kernels, local(): pl.pallas_call(raw_kernel, in_specs=[smem] + [anywhere] * 14, out_specs=v...  7.78 us
    pallas_call x1, Pallas kernels, local(): pl.pallas_call(gate_kernel, in_specs=[smem] + [anywhere] * 13, out_specs=...  7.5 us
  transfers between devices with their start and end apart: 38, of which 18 were waited for; matrix products, arithmetic and copies ran while one was open for 7% of the time, Pallas kernels for 22%

profile of v4, /device:TPU:1, one launch (start us, length us, event | category | flops | bytes accessed | tf_op | source)
XLA Modules:
  0.0 229.3 jit_solution(15255811080521969676)
XLA Ops:
  6.5 1.8 pad_maximum_fusion.2
  8.4 3.6 %collective-permute-start.5 = (bf16[128,256]{1,0:T(8,128)(2,1)}, bf16[128,256]{1,0:T(8,128)(2,1)S(1)}, u32[]{:S(2)}, u32[]{:S(2)}) collective-permute-start(bf16[128,256]{1,0:T(8,128)(2,1)} %param.14), channel_id=1, source_target_pairs={{8,0},{16,8},{24,16},{0,24},{9,1},{17,9},{25,17},{1,25},{10,2},{18... | collective-permute-start | bytes 196616 | tf_op jit(solution)/shard_map/ppermute | solution.py:275
  14.0 3.0 %collective-permute-done.6 = bf16[128,256]{1,0:T(8,128)(2,1)S(1)} collective-permute-done((bf16[128,256]{1,0:T(8,128)(2,1)}, bf16[128,256]{1,0:T(8,128)(2,1)S(1)}, u32[]{:S(2)}, u32[]{:S(2)}) %collective-permute-start.6) | collective-permute-done | bytes 65568 | tf_op jit(solution)/shard_map/ppermute | solution.py:275
  21.5 2.6 %collective-permute-start.1 = (bf16[784,512]{1,0:T(8,128)(2,1)S(1)}, bf16[784,512]{1,0:T(8,128)(2,1)S(1)}, u32[]{:S(2)}, u32[]{:S(2)}) collective-permute-start(bf16[784,512]{1,0:T(8,128)(2,1)S(1)} %constant_dynamic-update-slice_fusion.refs_0_), channel_id=1, source_target_pairs={{2,0},{4,2},{6,4},{0,6},{3,1},{5,3},{7,5},{1,7},{10,8},{12,10},{14... | collective-permute-start | bytes 2408456 | tf_op jit(solution)/shard_map/ppermute | solution.py:275
  24.0 11.6 %collective-permute-start.8 = (bf16[512,128]{1,0:T(8,128)(2,1)S(1)}, bf16[512,128]{1,0:T(8,128)(2,1)S(1)}, u32[]{:S(2)}, u32[]{:S(2)}) collective-permute-start(bf16[512,128]{1,0:T(8,128)(2,1)S(1)} %copy-done.19), channel_id=1, source_target_pairs={{0,0},{1,32},{32,1},{33,33},{64,64},{65,96},{96,65},{97,97},{128,1... | collective-permute-start | bytes 393224 | tf_op jit(solution)/shard_map/ppermute | solution.py:313
  35.6 4.6 %collective-permute-done.8 = bf16[512,128]{1,0:T(8,128)(2,1)S(1)} collective-permute-done((bf16[512,128]{1,0:T(8,128)(2,1)S(1)}, bf16[512,128]{1,0:T(8,128)(2,1)S(1)}, u32[]{:S(2)}, u32[]{:S(2)}) %collective-permute-start.8) | collective-permute-done | bytes 131104 | tf_op jit(solution)/shard_map/ppermute | solution.py:313
  40.8 4.4 %collective-permute-done.9 = bf16[512,128]{1,0:T(8,128)(2,1)S(1)} collective-permute-done((bf16[512,128]{1,0:T(8,128)(2,1)S(1)}, bf16[512,128]{1,0:T(8,128)(2,1)S(1)}, u32[]{:S(2)}, u32[]{:S(2)}) %collective-permute-start.9) | collective-permute-done | bytes 131104 | tf_op jit(solution)/shard_map/ppermute | solution.py:275
  45.2 1.6 collective-permute-done.10
  46.9 1.6 collective-permute-start.13
  48.6 2.1 collective-permute-done.11
  50.8 4.2 %collective-permute-start.3 = (bf16[400,512]{1,0:T(8,128)(2,1)S(1)}, bf16[400,512]{1,0:T(8,128)(2,1)}, u32[]{:S(2)}, u32[]{:S(2)}) collective-permute-start(bf16[400,512]{1,0:T(8,128)(2,1)S(1)} %slice.32), channel_id=1, source_target_pairs={{2,0},{4,2},{6,4},{0,6},{3,1},{5,3},{7,5},{1,7},{10,8},{12,10},{14... | collective-permute-start | bytes 1228808 | tf_op jit(solution)/shard_map/ppermute | solution.py:275
  56.2 9.9 %collective-permute-done.4 = bf16[384,512]{1,0:T(8,128)(2,1)} collective-permute-done((bf16[384,512]{1,0:T(8,128)(2,1)S(1)}, bf16[384,512]{1,0:T(8,128)(2,1)}, u32[]{:S(2)}, u32[]{:S(2)}) %collective-permute-start.4) | collective-permute-done | bytes 393248 | tf_op jit(solution)/shard_map/ppermute | solution.py:275
  67.4 2.3 %fusion = (bf16[4,128,512]{2,1,0:T(8,128)(2,1)}, bf16[4,128,512]{2,1,0:T(8,128)(2,1)}) fusion(bf16[8,128,1024]{2,1,0:T(8,128)(2,1)} %bitcast.24), kind=kLoop, calls=%fused_computation.31 | loop fusion | bytes 2097152 | tf_op jit(solution)/shard_map/slice | solution.py:328
  73.0 10.2 %collective-permute-done.16.refs_10_ = bf16[4,128,512]{2,1,0:T(8,128)(2,1)} collective-permute-done((bf16[4,128,512]{2,1,0:T(8,128)(2,1)}, bf16[4,128,512]{2,1,0:T(8,128)(2,1)}, u32[]{:S(2)}, u32[]{:S(2)}) %collective-permute-start.16) | collective-permute-done | bytes 524320 | tf_op jit(solution)/shard_map/ppermute | solution.py:275
  86.7 7.7 %collective-permute-done.20.refs_11_ = bf16[4,128,512]{2,1,0:T(8,128)(2,1)} collective-permute-done((bf16[4,128,512]{2,1,0:T(8,128)(2,1)}, bf16[4,128,512]{2,1,0:T(8,128)(2,1)}, u32[]{:S(2)}, u32[]{:S(2)}) %collective-permute-start.20) | collective-permute-done | bytes 524320 | tf_op jit(solution)/shard_map/ppermute | solution.py:275
  96.8 7.8 %raw.1.refs_11_ = f32[784,512]{1,0:T(8,128)} custom-call(s32[4]{0:T(128)} %pad_add_fusion.1.place, bf16[784,512]{1,0:T(8,128)(2,1)} %copy-done.5, bf16[784,512]{1,0:T(8,128)(2,1)} %copy-done.2, bf16[784,512]{1,0:T(8,128)(2,1)} %copy-done, bf16[784,512]{1,0:T(8,128)(2,1)} %copy-done.3, bf16[784,512]{1,0:T(8,128)(2,1)} %collective-permute-done.12.refs_4_, ...), custom_call_target="tpu_custom_call" | custom-call | flops 3221225472 | bytes 9437184 | tf_op jit(solution)/shard_map/raw/pallas_call | solution.py:347
  109.3 12.4 %conv.1 = (bf16[768,768]{1,0:T(8,128)(2,1)}, bf16[32,8,512]{2,1,0:T(8,128)(2,1)}) custom-call(s32[4]{0:T(128)} %pad_add_fusion.1.place, bf16[784,512]{1,0:T(8,128)(2,1)} %copy-done.5, bf16[784,512]{1,0:T(8,128)(2,1)} %copy-done.2, bf16[784,512]{1,0:T(8,128)(2,1)} %copy-done, bf16[784,512]{1,0:T(8,128)(2,1)} %copy-done.3, ...), custom_call_target="tpu_custom_call" | custom-call | tf_op jit(solution)/shard_map/conv/pallas_call | solution.py:364
  121.7 21.1 %all-to-all-start = ((bf16[32,8,512]{2,1,0:T(8,128)(2,1)}), bf16[32,8,512]{2,1,0:T(8,128)(2,1)S(1)}, u32[]{:S(2)}, u32[]{:S(2)}) async-start(bf16[32,8,512]{2,1,0:T(8,128)(2,1)} %get-tuple-element.37), calls=%async_computation | async-start | bytes 524288 | tf_op jit(solution)/shard_map/all_to_all | solution.py:388
  142.9 2.4 %collective-permute-start.24 = (bf16[4,128,512]{2,1,0:T(8,128)(2,1)S(1)}, bf16[4,128,512]{2,1,0:T(8,128)(2,1)S(1)}, u32[]{:S(2)}, u32[]{:S(2)}) collective-permute-start(bf16[4,128,512]{2,1,0:T(8,128)(2,1)S(1)} %slice.30), channel_id=1, source_target_pairs={{8,0},{16,8},{24,16},{0,24},{9,1},{17,9},{25,17},{1,25},{10,2},{18... | collective-permute-start | bytes 1572872 | tf_op jit(solution)/shard_map/ppermute | solution.py:275
  147.2 6.2 %scan.1.earlier.output = f32[768,512]{1,0:T(8,128)} custom-call(bf16[768,768]{1,0:T(8,128)(2,1)} %get-tuple-element.36.conv, f32[8,768]{1,0:T(8,128)} %bitcast.27, f32[8,1]{1,0:T(8,128)} %copy.12.refs_15_.rate, f32[8,1]{1,0:T(8,128)} %copy.14.skip), custom_call_target="tpu_custom_call" | custom-call | tf_op jit(solution)/shard_map/scan/pallas_call | solution.py:391
  153.3 3.7 %all-to-all-done.states = bf16[32,8,512]{2,1,0:T(8,128)(2,1)S(1)} async-done(((bf16[32,8,512]{2,1,0:T(8,128)(2,1)}), bf16[32,8,512]{2,1,0:T(8,128)(2,1)S(1)}, u32[]{:S(2)}, u32[]{:S(2)}) %all-to-all-start) | async-done | bytes 262176 | tf_op jit(solution)/shard_map/all_to_all | solution.py:388
  157.8 1.8 prefix.1
  159.6 5.4 %all-to-all-start.1 = ((bf16[32,4,512]{2,1,0:T(4,128)(2,1)}), bf16[32,4,512]{2,1,0:T(4,128)(2,1)S(1)}, u32[]{:S(2)}, u32[]{:S(2)}) async-start(bf16[32,4,512]{2,1,0:T(4,128)(2,1)} %prefix.1), calls=%async_computation.1 | async-start | bytes 262144 | tf_op jit(solution)/shard_map/all_to_all | solution.py:406
  166.7 7.5 %gate.1 = bf16[768,512]{1,0:T(8,128)(2,1)} custom-call(s32[4]{0:T(128)} %pad_add_fusion.1.place, bf16[784,512]{1,0:T(8,128)(2,1)} %copy-done.5, bf16[784,512]{1,0:T(8,128)(2,1)} %copy-done.2, bf16[784,512]{1,0:T(8,128)(2,1)} %copy-done, bf16[784,512]{1,0:T(8,128)(2,1)} %copy-done.3, bf16[784,512]{1,0:T(8,128)(2,1)} %collective-permute-done.12.refs_4_, ...), custom_call_target="tpu_custom_call" | custom-call | tf_op jit(solution)/shard_map/gate/pallas_call | solution.py:408
  175.0 4.9 %norm.1.own.earlier = bf16[768,512]{1,0:T(8,128)(2,1)} custom-call(f32[768,512]{1,0:T(8,128)} %scan.1.earlier.output, bf16[768,768]{1,0:T(8,128)(2,1)} %get-tuple-element.36.conv, f32[8,768]{1,0:T(8,128)} %bitcast.28, f32[8,1]{1,0:T(8,128)} %copy.12.refs_15_.rate, bf16[32,4,512]{2,1,0:T(4,128)(2,1)} %copy-done.16, bf16[768,512]{1,0:T(8,128)(2,1)} %gate.1, ...), custom_call_target="tpu_custom_call" | custom-call | tf_op jit(solution)/shard_map/norm/pallas_call | solution.py:424
  179.8 4.0 %collective-permute-start.26 = (bf16[768,512]{1,0:T(8,128)(2,1)}, bf16[768,512]{1,0:T(8,128)(2,1)S(1)}, u32[]{:S(2)}, u32[]{:S(2)}) collective-permute-start(bf16[768,512]{1,0:T(8,128)(2,1)} %norm.1.own.earlier), channel_id=1, source_target_pairs={{1,0},{0,1},{3,2},{2,3},{5,4},{4,5},{7,6},{6,7},{9,8},{8,9},{11,10... | collective-permute-start | bytes 2359304 | tf_op jit(solution)/shard_map/ppermute | solution.py:275
  186.8 4.1 %out.3 = (bf16[384,512]{1,0:T(8,128)(2,1)}, bf16[384,512]{1,0:T(8,128)(2,1)}) custom-call(s32[2]{0:T(128)} %pad_add_fusion.3.targets, bf16[768,512]{1,0:T(8,128)(2,1)} %norm.1.own.earlier, bf16[768,512]{1,0:T(8,128)(2,1)} %copy-done.1, bf16[8,512,512]{2,1,0:T(8,128)(2,1)} %bitcast.18, bf16[8,512,512]{2,1,0:T(8,128)(2,1)} %bitcast.19, ...), custom_call_target="tpu_custom_call" | custom-call | flops 805306368 | bytes 1048576 | tf_op jit(solution)/shard_map/out/pallas_call | solution.py:440
  191.5 2.7 %collective-permute-start.31 = (bf16[384,512]{1,0:T(8,128)(2,1)}, bf16[384,512]{1,0:T(8,128)(2,1)S(1)}, u32[]{:S(2)}, u32[]{:S(2)}) collective-permute-start(bf16[384,512]{1,0:T(8,128)(2,1)} %get-tuple-element.50), channel_id=1, source_target_pairs={{2,0},{4,2},{6,4},{0,6},{3,1},{5,3},{7,5},{1,7},{10,8},{12,10},{14... | collective-permute-start | bytes 1179656 | tf_op jit(solution)/shard_map/ppermute | solution.py:275
  194.2 6.3 %out.4 = (f32[384,512]{1,0:T(8,128)}, bf16[384,512]{1,0:T(8,128)(2,1)}, bf16[384,512]{1,0:T(8,128)(2,1)}, f32[384,512]{1,0:T(8,128)}) custom-call(s32[4]{0:T(128)} %pad_add_fusion.2.targets, bf16[768,512]{1,0:T(8,128)(2,1)} %norm.1.own.earlier, bf16[768,512]{1,0:T(8,128)(2,1)} %copy-done.1, bf16[8,512,512]{2,1,0:T(8,128)(2,1)} %bitcast.20, ...), custom_call_target="tpu_custom_call" | custom-call | flops 1610612736 | bytes 2097152 | tf_op jit(solution)/shard_map/out/pallas_call | solution.py:440
  204.1 2.7 %collective-permute-start.32 = (bf16[384,512]{1,0:T(8,128)(2,1)S(1)}, bf16[384,512]{1,0:T(8,128)(2,1)S(1)}, u32[]{:S(2)}, u32[]{:S(2)}) collective-permute-start(bf16[384,512]{1,0:T(8,128)(2,1)S(1)} %add_convert_fusion.1), channel_id=1, source_target_pairs={{2,0},{4,2},{6,4},{0,6},{3,1},{5,3},{7,5},{1,7},{10,8},{12,10},{14... | collective-permute-start | bytes 1179656 | tf_op jit(solution)/shard_map/ppermute | solution.py:275
  207.5 4.2 %out.5 = (f32[384,512]{1,0:T(8,128)}, f32[384,512]{1,0:T(8,128)}) custom-call(s32[2]{0:T(128)} %pad_add_fusion.targets, bf16[768,512]{1,0:T(8,128)(2,1)} %norm.1.own.earlier, bf16[768,512]{1,0:T(8,128)(2,1)} %copy-done.1, bf16[8,512,512]{2,1,0:T(8,128)(2,1)} %bitcast.22, bf16[8,512,512]{2,1,0:T(8,128)(2,1)} %bitcast.23, bf16[384,512]{1,0:T(8,128)(2,1)} %copy-done.8), custom_call_target="tpu_custom_call" | custom-call | flops 805306368 | bytes 1048576 | tf_op jit(solution)/shard_map/out/pallas_call | solution.py:440
  211.7 8.4 %collective-permute-done.29 = bf16[384,512]{1,0:T(8,128)(2,1)S(1)} collective-permute-done((bf16[384,512]{1,0:T(8,128)(2,1)S(1)}, bf16[384,512]{1,0:T(8,128)(2,1)S(1)}, u32[]{:S(2)}, u32[]{:S(2)}) %collective-permute-start.29) | collective-permute-done | bytes 393248 | tf_op jit(solution)/shard_map/ppermute | solution.py:275
  (136 shorter events, 38.8 us)
Async XLA Ops:
  6.5 60.8 %all-gather.8.cloned.1.call-start = ((), (), s32[]{:S(2)}) async-start(), calls=%async_computation.3 | async-start | bytes 2359296 | tf_op jit(solution)/shard_map/all_gather | solution.py:307
  8.3 101.0 %all-gather.6.cloned.1.call-start = ((), (), s32[]{:S(2)}) async-start(), calls=%async_computation.2 | async-start | bytes 2359296 | tf_op jit(solution)/shard_map/all_gather | solution.py:323
  19.2 166.8 %all-gather.10.cloned.1.call-start = ((), (), s32[]{:S(2)}) async-start(), calls=%async_computation.4 | async-start | bytes 4718592 | tf_op jit(solution)/shard_map/all_gather | solution.py:335
  21.5 25.4 %collective-permute-start.1 = (bf16[784,512]{1,0:T(8,128)(2,1)S(1)}, bf16[784,512]{1,0:T(8,128)(2,1)S(1)}, u32[]{:S(2)}, u32[]{:S(2)}) collective-permute-start(bf16[784,512]{1,0:T(8,128)(2,1)S(1)} %constant_dynamic-update-slice_fusion.refs_0_), channel_id=1, source_target_pairs={{2,0},{4,2},{6,4},{0,6},{3,1},{5,3},{7,5},{1,7},{10,8},{12,10},{14... | collective-permute-start | bytes 2408456 | tf_op jit(solution)/shard_map/ppermute | solution.py:275
  24.0 24.4 %collective-permute-start.2 = (bf16[784,512]{1,0:T(8,128)(2,1)S(1)}, bf16[784,512]{1,0:T(8,128)(2,1)S(1)}, u32[]{:S(2)}, u32[]{:S(2)}) collective-permute-start(bf16[784,512]{1,0:T(8,128)(2,1)S(1)} %constant_dynamic-update-slice_fusion.refs_0_), channel_id=1, source_target_pairs={{6,0},{0,2},{2,4},{4,6},{7,1},{1,3},{3,5},{5,7},{14,8},{8,10},{10,... | collective-permute-start | bytes 2408456 | tf_op jit(solution)/shard_map/ppermute | solution.py:275
  24.0 16.2 %collective-permute-start.8 = (bf16[512,128]{1,0:T(8,128)(2,1)S(1)}, bf16[512,128]{1,0:T(8,128)(2,1)S(1)}, u32[]{:S(2)}, u32[]{:S(2)}) collective-permute-start(bf16[512,128]{1,0:T(8,128)(2,1)S(1)} %copy-done.19), channel_id=1, source_target_pairs={{0,0},{1,32},{32,1},{33,33},{64,64},{65,96},{96,65},{97,97},{128,1... | collective-permute-start | bytes 393224 | tf_op jit(solution)/shard_map/ppermute | solution.py:313
  40.8 26.5 %collective-permute-start.12 = (bf16[784,512]{1,0:T(8,128)(2,1)S(1)}, bf16[784,512]{1,0:T(8,128)(2,1)}, u32[]{:S(2)}, u32[]{:S(2)}) collective-permute-start(bf16[784,512]{1,0:T(8,128)(2,1)S(1)} %constant_dynamic-update-slice_fusion.refs_0_), channel_id=1, source_target_pairs={{1,0},{0,1},{3,2},{2,3},{5,4},{4,5},{7,6},{6,7},{9,8},{8,9},{11,10... | collective-permute-start | bytes 2408456 | tf_op jit(solution)/shard_map/ppermute | solution.py:275
  40.8 6.1 %collective-permute-start.10 = (bf16[512,128]{1,0:T(8,128)(2,1)S(1)}, bf16[512,128]{1,0:T(8,128)(2,1)S(1)}, u32[]{:S(2)}, u32[]{:S(2)}) collective-permute-start(bf16[512,128]{1,0:T(8,128)(2,1)S(1)} %collective-permute-done.8), channel_id=1, source_target_pairs={{16,0},{24,8},{0,16},{8,24},{17,1},{25,9},{1,17},{9,25},{18,2},{26... | collective-permute-start | bytes 393224 | tf_op jit(solution)/shard_map/ppermute | solution.py:275
  46.9 20.4 %collective-permute-start.13 = (bf16[784,512]{1,0:T(8,128)(2,1)S(1)}, bf16[784,512]{1,0:T(8,128)(2,1)}, u32[]{:S(2)}, u32[]{:S(2)}) collective-permute-start(bf16[784,512]{1,0:T(8,128)(2,1)S(1)} %collective-permute-done.1.refs_1_), channel_id=1, source_target_pairs={{1,0},{0,1},{3,2},{2,3},{5,4},{4,5},{7,6},{6,7},{9,8},{8,9},{11,10... | collective-permute-start | bytes 2408456 | tf_op jit(solution)/shard_map/ppermute | solution.py:275
  48.4 18.8 %collective-permute-start.14 = (bf16[784,512]{1,0:T(8,128)(2,1)S(1)}, bf16[784,512]{1,0:T(8,128)(2,1)}, u32[]{:S(2)}, u32[]{:S(2)}) collective-permute-start(bf16[784,512]{1,0:T(8,128)(2,1)S(1)} %collective-permute-done.2.refs_3_), channel_id=1, source_target_pairs={{1,0},{0,1},{3,2},{2,3},{5,4},{4,5},{7,6},{6,7},{9,8},{8,9},{11,10... | collective-permute-start | bytes 2408456 | tf_op jit(solution)/shard_map/ppermute | solution.py:275
  50.8 15.2 %collective-permute-start.3 = (bf16[400,512]{1,0:T(8,128)(2,1)S(1)}, bf16[400,512]{1,0:T(8,128)(2,1)}, u32[]{:S(2)}, u32[]{:S(2)}) collective-permute-start(bf16[400,512]{1,0:T(8,128)(2,1)S(1)} %slice.32), channel_id=1, source_target_pairs={{2,0},{4,2},{6,4},{0,6},{3,1},{5,3},{7,5},{1,7},{10,8},{12,10},{14... | collective-permute-start | bytes 1228808 | tf_op jit(solution)/shard_map/ppermute | solution.py:275
  55.1 11.0 %collective-permute-start.4 = (bf16[384,512]{1,0:T(8,128)(2,1)S(1)}, bf16[384,512]{1,0:T(8,128)(2,1)}, u32[]{:S(2)}, u32[]{:S(2)}) collective-permute-start(bf16[384,512]{1,0:T(8,128)(2,1)S(1)} %slice.33), channel_id=1, source_target_pairs={{6,0},{0,2},{2,4},{4,6},{7,1},{1,3},{3,5},{5,7},{14,8},{8,10},{10,... | collective-permute-start | bytes 1179656 | tf_op jit(solution)/shard_map/ppermute | solution.py:275
  67.3 28.6 %collective-permute-start.15 = (bf16[784,512]{1,0:T(8,128)(2,1)S(1)}, bf16[784,512]{1,0:T(8,128)(2,1)S(1)}, u32[]{:S(2)}, u32[]{:S(2)}) collective-permute-start(bf16[784,512]{1,0:T(8,128)(2,1)S(1)} %pad_maximum_fusion.refs_2_), channel_id=1, source_target_pairs={{1,0},{0,1},{3,2},{2,3},{5,4},{4,5},{7,6},{6,7},{9,8},{8,9},{11,10... | collective-permute-start | bytes 2408456 | tf_op jit(solution)/shard_map/ppermute | solution.py:275
  69.8 13.4 %collective-permute-start.16 = (bf16[4,128,512]{2,1,0:T(8,128)(2,1)}, bf16[4,128,512]{2,1,0:T(8,128)(2,1)}, u32[]{:S(2)}, u32[]{:S(2)}) collective-permute-start(bf16[4,128,512]{2,1,0:T(8,128)(2,1)} %get-tuple-element.52.refs_8_), channel_id=1, source_target_pairs={{8,0},{16,8},{24,16},{0,24},{9,1},{17,9},{25,17},{1,25},{10,2},{18... | collective-permute-start | bytes 1572872 | tf_op jit(solution)/shard_map/ppermute | solution.py:275
  70.1 14.6 %collective-permute-start.18 = (bf16[4,128,512]{2,1,0:T(8,128)(2,1)}, bf16[4,128,512]{2,1,0:T(8,128)(2,1)}, u32[]{:S(2)}, u32[]{:S(2)}) collective-permute-start(bf16[4,128,512]{2,1,0:T(8,128)(2,1)} %get-tuple-element.51.refs_9_), channel_id=1, source_target_pairs={{24,0},{0,8},{8,16},{16,24},{25,1},{1,9},{9,17},{17,25},{26,2},{2,... | collective-permute-start | bytes 1572872 | tf_op jit(solution)/shard_map/ppermute | solution.py:275
  71.5 23.0 %collective-permute-start.20 = (bf16[4,128,512]{2,1,0:T(8,128)(2,1)}, bf16[4,128,512]{2,1,0:T(8,128)(2,1)}, u32[]{:S(2)}, u32[]{:S(2)}) collective-permute-start(bf16[4,128,512]{2,1,0:T(8,128)(2,1)} %get-tuple-element.51.refs_9_), channel_id=1, source_target_pairs={{8,0},{16,8},{24,16},{0,24},{9,1},{17,9},{25,17},{1,25},{10,2},{18... | collective-permute-start | bytes 1572872 | tf_op jit(solution)/shard_map/ppermute | solution.py:275
  73.0 22.9 %collective-permute-start.21 = (bf16[4,128,512]{2,1,0:T(8,128)(2,1)}, bf16[4,128,512]{2,1,0:T(8,128)(2,1)}, u32[]{:S(2)}, u32[]{:S(2)}) collective-permute-start(bf16[4,128,512]{2,1,0:T(8,128)(2,1)} %get-tuple-element.52.refs_8_), channel_id=1, source_target_pairs={{24,0},{0,8},{8,16},{16,24},{25,1},{1,9},{9,17},{17,25},{26,2},{2,... | collective-permute-start | bytes 1572872 | tf_op jit(solution)/shard_map/ppermute | solution.py:275
  83.2 22.5 %collective-permute-start.17 = (bf16[4,128,512]{2,1,0:T(8,128)(2,1)}, bf16[4,128,512]{2,1,0:T(8,128)(2,1)S(1)}, u32[]{:S(2)}, u32[]{:S(2)}) collective-permute-start(bf16[4,128,512]{2,1,0:T(8,128)(2,1)} %collective-permute-done.16.refs_10_), channel_id=1, source_target_pairs={{8,0},{16,8},{24,16},{0,24},{9,1},{17,9},{25,17},{1,25},{10,2},{18... | collective-permute-start | bytes 1572872 | tf_op jit(solution)/shard_map/ppermute | solution.py:275
  84.8 22.4 %collective-permute-start.19 = (bf16[4,128,512]{2,1,0:T(8,128)(2,1)}, bf16[4,128,512]{2,1,0:T(8,128)(2,1)}, u32[]{:S(2)}, u32[]{:S(2)}) collective-permute-start(bf16[4,128,512]{2,1,0:T(8,128)(2,1)} %collective-permute-done.18.refs_13_), channel_id=1, source_target_pairs={{24,0},{0,8},{8,16},{16,24},{25,1},{1,9},{9,17},{17,25},{26,2},{2,... | collective-permute-start | bytes 1572872 | tf_op jit(solution)/shard_map/ppermute | solution.py:275
  107.1 35.7 %collective-permute-start.22 = (bf16[8,128,512]{2,1,0:T(8,128)(2,1)S(1)}, bf16[8,128,512]{2,1,0:T(8,128)(2,1)S(1)}, u32[]{:S(2)}, u32[]{:S(2)}) collective-permute-start(bf16[8,128,512]{2,1,0:T(8,128)(2,1)S(1)} %slice.29.refs_8_), channel_id=1, source_target_pairs={{8,0},{16,8},{24,16},{0,24},{9,1},{17,9},{25,17},{1,25},{10,2},{18... | collective-permute-start | bytes 3145736 | tf_op jit(solution)/shard_map/ppermute | solution.py:275
  107.9 35.0 %collective-permute-start.23 = (bf16[8,128,512]{2,1,0:T(8,128)(2,1)S(1)}, bf16[8,128,512]{2,1,0:T(8,128)(2,1)}, u32[]{:S(2)}, u32[]{:S(2)}) collective-permute-start(bf16[8,128,512]{2,1,0:T(8,128)(2,1)S(1)} %slice.29.refs_8_), channel_id=1, source_target_pairs={{24,0},{0,8},{8,16},{16,24},{25,1},{1,9},{9,17},{17,25},{26,2},{2,... | collective-permute-start | bytes 3145736 | tf_op jit(solution)/shard_map/ppermute | solution.py:275
  121.7 35.3 %all-to-all-start = ((bf16[32,8,512]{2,1,0:T(8,128)(2,1)}), bf16[32,8,512]{2,1,0:T(8,128)(2,1)S(1)}, u32[]{:S(2)}, u32[]{:S(2)}) async-start(bf16[32,8,512]{2,1,0:T(8,128)(2,1)} %get-tuple-element.37), calls=%async_computation | async-start | bytes 524288 | tf_op jit(solution)/shard_map/all_to_all | solution.py:388
  142.9 22.1 %collective-permute-start.24 = (bf16[4,128,512]{2,1,0:T(8,128)(2,1)S(1)}, bf16[4,128,512]{2,1,0:T(8,128)(2,1)S(1)}, u32[]{:S(2)}, u32[]{:S(2)}) collective-permute-start(bf16[4,128,512]{2,1,0:T(8,128)(2,1)S(1)} %slice.30), channel_id=1, source_target_pairs={{8,0},{16,8},{24,16},{0,24},{9,1},{17,9},{25,17},{1,25},{10,2},{18... | collective-permute-start | bytes 1572872 | tf_op jit(solution)/shard_map/ppermute | solution.py:275
  146.4 18.6 %collective-permute-start.25 = (bf16[4,128,512]{2,1,0:T(8,128)(2,1)S(1)}, bf16[4,128,512]{2,1,0:T(8,128)(2,1)S(1)}, u32[]{:S(2)}, u32[]{:S(2)}) collective-permute-start(bf16[4,128,512]{2,1,0:T(8,128)(2,1)S(1)} %slice.31), channel_id=1, source_target_pairs={{24,0},{0,8},{8,16},{16,24},{25,1},{1,9},{9,17},{17,25},{26,2},{2,... | collective-permute-start | bytes 1572872 | tf_op jit(solution)/shard_map/ppermute | solution.py:275
  159.6 14.8 %all-to-all-start.1 = ((bf16[32,4,512]{2,1,0:T(4,128)(2,1)}), bf16[32,4,512]{2,1,0:T(4,128)(2,1)S(1)}, u32[]{:S(2)}, u32[]{:S(2)}) async-start(bf16[32,4,512]{2,1,0:T(4,128)(2,1)} %prefix.1), calls=%async_computation.1 | async-start | bytes 262144 | tf_op jit(solution)/shard_map/all_to_all | solution.py:406
  179.8 6.1 %collective-permute-start.26 = (bf16[768,512]{1,0:T(8,128)(2,1)}, bf16[768,512]{1,0:T(8,128)(2,1)S(1)}, u32[]{:S(2)}, u32[]{:S(2)}) collective-permute-start(bf16[768,512]{1,0:T(8,128)(2,1)} %norm.1.own.earlier), channel_id=1, source_target_pairs={{1,0},{0,1},{3,2},{2,3},{5,4},{4,5},{7,6},{6,7},{9,8},{8,9},{11,10... | collective-permute-start | bytes 2359304 | tf_op jit(solution)/shard_map/ppermute | solution.py:275
  190.9 11.8 %collective-permute-start.27 = (bf16[384,512]{1,0:T(8,128)(2,1)}, bf16[384,512]{1,0:T(8,128)(2,1)S(1)}, u32[]{:S(2)}, u32[]{:S(2)}) collective-permute-start(bf16[384,512]{1,0:T(8,128)(2,1)} %get-tuple-element.43.earlier), channel_id=1, source_target_pairs={{6,0},{0,2},{2,4},{4,6},{7,1},{1,3},{3,5},{5,7},{14,8},{8,10},{10,... | collective-permute-start | bytes 1179656 | tf_op jit(solution)/shard_map/ppermute | solution.py:275
  191.5 12.5 %collective-permute-start.31 = (bf16[384,512]{1,0:T(8,128)(2,1)}, bf16[384,512]{1,0:T(8,128)(2,1)S(1)}, u32[]{:S(2)}, u32[]{:S(2)}) collective-permute-start(bf16[384,512]{1,0:T(8,128)(2,1)} %get-tuple-element.50), channel_id=1, source_target_pairs={{2,0},{4,2},{6,4},{0,6},{3,1},{5,3},{7,5},{1,7},{10,8},{12,10},{14... | collective-permute-start | bytes 1179656 | tf_op jit(solution)/shard_map/ppermute | solution.py:275
  200.5 11.2 %collective-permute-start.28 = (bf16[384,512]{1,0:T(8,128)(2,1)}, bf16[384,512]{1,0:T(8,128)(2,1)S(1)}, u32[]{:S(2)}, u32[]{:S(2)}) collective-permute-start(bf16[384,512]{1,0:T(8,128)(2,1)} %get-tuple-element.46), channel_id=1, source_target_pairs={{2,0},{4,2},{6,4},{0,6},{3,1},{5,3},{7,5},{1,7},{10,8},{12,10},{14... | collective-permute-start | bytes 1179656 | tf_op jit(solution)/shard_map/ppermute | solution.py:275
  200.5 20.9 %collective-permute-start.30 = (bf16[384,512]{1,0:T(8,128)(2,1)}, bf16[384,512]{1,0:T(8,128)(2,1)S(1)}, u32[]{:S(2)}, u32[]{:S(2)}) collective-permute-start(bf16[384,512]{1,0:T(8,128)(2,1)} %get-tuple-element.48), channel_id=1, source_target_pairs={{6,0},{0,2},{2,4},{4,6},{7,1},{1,3},{3,5},{5,7},{14,8},{8,10},{10,... | collective-permute-start | bytes 1179656 | tf_op jit(solution)/shard_map/ppermute | solution.py:275
  203.9 16.2 %collective-permute-start.29 = (bf16[384,512]{1,0:T(8,128)(2,1)S(1)}, bf16[384,512]{1,0:T(8,128)(2,1)S(1)}, u32[]{:S(2)}, u32[]{:S(2)}) collective-permute-start(bf16[384,512]{1,0:T(8,128)(2,1)S(1)} %add_convert_fusion.3.earlier), channel_id=1, source_target_pairs={{6,0},{0,2},{2,4},{4,6},{7,1},{1,3},{3,5},{5,7},{14,8},{8,10},{10,... | collective-permute-start | bytes 1179656 | tf_op jit(solution)/shard_map/ppermute | solution.py:275
  204.1 17.3 %collective-permute-start.32 = (bf16[384,512]{1,0:T(8,128)(2,1)S(1)}, bf16[384,512]{1,0:T(8,128)(2,1)S(1)}, u32[]{:S(2)}, u32[]{:S(2)}) collective-permute-start(bf16[384,512]{1,0:T(8,128)(2,1)S(1)} %add_convert_fusion.1), channel_id=1, source_target_pairs={{2,0},{4,2},{6,4},{0,6},{3,1},{5,3},{7,5},{1,7},{10,8},{12,10},{14... | collective-permute-start | bytes 1179656 | tf_op jit(solution)/shard_map/ppermute | solution.py:275
  (26 other events, 225.0 us)
Sparse Core Ops, SparseCore 0:
  9.1 41.9 all-gather.7
  52.9 39.4 all-gather.5
  94.2 62.2 all-gather.9
